TPU v7x, 32 devices: a whole 2x2x4 slice. The times are simulated.
32 devices in a mesh: gx: 8 (over z, x), gy: 4 (over y, core).
Axes of the slice: x: 2, y: 2, z: 4, core: 2. Of those that a mesh axis runs over, the one named last changes fastest.
Arguments:
- a_blocks: bfloat16 [8, 32, 64, 448], P('gx', 'gy'), may hold values from -0.25 to 0.25
- a_cols: int32 [8, 32, 7], P('gx', 'gy'), may hold values from 0 to 15
- mushy: int32 [8, 32], P('gx', 'gy'), may hold values 0 or 1
- p_blocks: bfloat16 [8, 32, 64, 256], P('gx', 'gy'), may hold values from -0.375 to 0.375
- p_cols: int32 [8, 32, 4], P('gx', 'gy'), may hold values from 0 to 7
- send_rows: int32 [8, 32], P('gx', 'gy'), may hold values from 0 to 7
Outputs:
- coarse_tiles: float32 [8, 512, 1536], P('gx', 'gy')
All inputs are finite; a program needn't handle non-finite values. No bound on the sum of `mushy` on one device may be relied on, other than what follows from the above.
Results may differ from a plain program's by a relative error of at most 0.0038.
Values may be sent and summed in bfloat16 or wider, within the bound.
No kernel may reach another device: no remote copies, remote signals or barrier semaphores. Data moves between devices by JAX's collectives and lax.ppermute only.
A program may use at most 64 MiB of HBM per device.

v0:
```python
import functools

import jax
import jax.numpy as jnp
from jax import lax
from jax.experimental import pallas as pl
from jax.experimental.pallas import tpu as pltpu
from jax.sharding import PartitionSpec as P

KA = 7
KS = 3
INFO = 128
NCOL = 8
LANES = 128
WIDE = 256

F32 = jnp.float32
BF16 = jnp.bfloat16
SMEM = pl.BlockSpec(memory_space=pltpu.SMEM)
VMEM = pl.BlockSpec(memory_space=pltpu.VMEM)
HBM = pl.BlockSpec(memory_space=pltpu.HBM)
LONG = pl.CostEstimate(flops=10000000000, bytes_accessed=1000000, transcendentals=0)
MEDIUM = pl.CostEstimate(flops=1000000000, bytes_accessed=1000000, transcendentals=0)
SHORT = pl.CostEstimate(flops=100000000, bytes_accessed=1000000, transcendentals=0)
TINY = pl.CostEstimate(flops=1000000, bytes_accessed=1000000, transcendentals=0)
PARAMS = pltpu.CompilerParams(vmem_limit_bytes=24 * 1024 * 1024)


def spread(value, masks_of, width):
    size = value.shape[0]
    row = lax.broadcasted_iota(jnp.int32, (size, WIDE), 0)
    lane = lax.broadcasted_iota(jnp.int32, (size, WIDE), 1)
    unit = jnp.where(row == lane % size, 1.0, 0.0).astype(BF16)
    tiles = []
    for c in range(width // WIDE):
        moves = jnp.concatenate([unit * mask for mask in masks_of(c * WIDE // size)], axis=0)
        tiles.append(jnp.dot(value, moves, preferred_element_type=F32))
    return tiles


def masks_at(cols, size, dtype):
    slots = (lax.broadcasted_iota(jnp.int32, (1, WIDE), 1) // size).astype(dtype)
    return lambda first: [
        jnp.where(slots == col - first, 1.0, 0.0).astype(BF16) for col in cols
    ]


def multiply(info, a_ref, base, ext_ref, prod_ref):
    rows, size = a_ref.shape[0], a_ref.shape[1]
    ext_ref[ext_ref.shape[0] - 1] = jnp.zeros(ext_ref.shape[1:], BF16)
    none = ext_ref.shape[0] - 1
    for n in range(rows):
        picks = []
        for k in range(KA):
            spot = info[n * INFO + k] - base
            good = (spot >= 0) & (spot < none)
            picks.append(jnp.where(good, spot, none))
        picked = jnp.concatenate([ext_ref[spot] for spot in picks], axis=0)
        value = jnp.dot(a_ref[n], picked, preferred_element_type=F32)
        prod_ref[n * size : (n + 1) * size, :] = value.astype(BF16)


def finish(ownt_ref, prod, keep_ref, send_ref):
    rows = ownt_ref.shape[0] // 2
    sent = jnp.dot(ownt_ref[rows:, :], prod, preferred_element_type=F32)
    send_ref[...] = sent.astype(BF16).reshape(send_ref.shape)
    kept = jnp.dot(ownt_ref[:rows, :], prod, preferred_element_type=F32)
    keep_ref[...] = kept.reshape(keep_ref.shape)


def pack_kernel(
    sends_in, pcol_in, acol_in, mush_in, p_in, first_ref, second_ref, info_out,
    sends, pcol, acol, mush, info, p_ref, packed_ref, sems,
):
    copies = [
        pltpu.make_async_copy(src, dst, sems.at[i])
        for i, (src, dst) in enumerate(
            ((sends_in, sends), (pcol_in, pcol), (acol_in, acol), (mush_in, mush), (p_in, p_ref))
        )
    ]
    for copy in copies:
        copy.start()
    for copy in copies[:4]:
        copy.wait()
    odd = lax.axis_index("gx") % 2
    rows, size = p_ref.shape[0], p_ref.shape[1]
    count = sends.shape[0] // 2
    slots = pcol.shape[0]
    for n in range(rows):
        limit = jnp.where(mush[n] > 0, KA, KS)
        for k in range(KA):
            info[n * INFO + k] = jnp.where(k < limit, acol[k, 0, n], -1)
        for j in range(slots):
            info[n * INFO + KA + j] = pcol[j, n]
    passed = pltpu.make_async_copy(info, info_out, sems.at[0])
    passed.start()
    starts = ((1 - odd) * count, odd * count)
    tail = packed_ref.shape[1] - count * size
    which = lax.broadcasted_iota(jnp.int32, (tail, packed_ref.shape[2]), 0)
    for i, start in enumerate(starts):
        cols = jnp.zeros(which.shape, F32)
        for s in range(count):
            row = sends[start + s]
            for j in range(slots):
                cols = jnp.where(which == s * slots + j, pcol[j, row].astype(F32), cols)
        packed_ref[i, count * size :, :] = cols.astype(BF16)
    copies[4].wait()
    copies = [passed]
    for i, (out_ref, start) in enumerate(zip((first_ref, second_ref), starts)):
        for s in range(count):
            packed_ref[i, s * size : (s + 1) * size, :] = p_ref[sends[start + s]]
        copies.append(pltpu.make_async_copy(packed_ref.at[i], out_ref, sems.at[1 + i]))
        copies[-1].start()
    for copy in copies:
        copy.wait()


def own_kernel(parts, info, a_ref, p_ref, ownt_ref, keep_ref, send_ref, own_ref, prod_ref):
    bit = lax.axis_index("gy") % 2
    rows, size = p_ref.shape[0], p_ref.shape[1]
    width = NCOL * size
    share = width // parts
    for n in range(rows):
        cols = [info[n * INFO + KA + j] for j in range(p_ref.shape[2] // size)]
        masks = masks_at(cols, size, jnp.int32)
        for c, tile in enumerate(spread(p_ref[n], masks, width)):
            own_ref[n, :, c * WIDE : (c + 1) * WIDE] = tile.astype(BF16)
    for c in range(width // LANES):
        column = own_ref[:rows, :, c * LANES : (c + 1) * LANES]
        flipped = column.reshape(rows * size, LANES).T
        for k in range(LANES // share):
            part = c * (LANES // share) + k
            spot = part // 2 + jnp.where(part % 2 == bit, 0, parts // 2)
            at = pl.ds(pl.multiple_of(spot * share, share), share)
            ownt_ref[at, :] = flipped[k * share : (k + 1) * share, :]
    multiply(info, a_ref, 0, own_ref, prod_ref)
    finish(ownt_ref, prod_ref[...], keep_ref, send_ref)


def scatter_kernel(when, info, a_ref, passed, *refs):
    high_ref, low_ref = refs[-3:-1] if when else refs[-2:]
    odd = lax.axis_index("gx") % 2
    rows, size = a_ref.shape[0], a_ref.shape[1]
    width = high_ref.shape[2]

    @pl.when(odd == when)
    def _():
        for n in range(rows):
            at = slice(n * size, (n + 1) * size)
            for order in range(2):
                right = odd if order else 1 - odd
                base = rows + right * (width // size)
                masks = masks_at([info[n * INFO + k] - base for k in range(KA)], size, jnp.int32)
                for c, tile in enumerate(spread(a_ref[n], masks, width)):
                    spot = slice(c * WIDE, (c + 1) * WIDE)
                    high = tile.astype(BF16)
                    high_ref[order, at, spot] = high
                    low_ref[order, at, spot] = (tile - high.astype(F32)).astype(BF16)


def ghost_kernel(order, high_ref, low_ref, in_ref, ownt_ref, *refs):
    keep_ref, send_ref, ext_ref, prod_ref = refs[-4:]
    width = ownt_ref.shape[0]
    size = width // NCOL
    slots = in_ref.shape[1] // size
    count = ext_ref.shape[0] // size
    cols = in_ref[count * size :, :].astype(F32)
    for n in range(count):
        at = slice(n * size, (n + 1) * size)
        masks = masks_at([cols[n * slots + j : n * slots + j + 1, :] for j in range(slots)], size, F32)
        for c, tile in enumerate(spread(in_ref[at, :], masks, width)):
            ext_ref[at, c * WIDE : (c + 1) * WIDE] = tile.astype(BF16)
    ext = ext_ref[...]
    step = prod_ref.shape[0] // 2
    for m in range(2):
        at = slice(m * step, (m + 1) * step)
        value = jnp.dot(high_ref[order, at, :], ext, preferred_element_type=F32)
        value += jnp.dot(low_ref[order, at, :], ext, preferred_element_type=F32)
        prod_ref[at, :] = value.astype(BF16)
    finish(ownt_ref, prod_ref[...], keep_ref, send_ref)


def fold_kernel(stage, keep_ref, recv_ref, *refs):
    next_ref, send_ref = refs[-2:]
    bit = (lax.axis_index("gy") >> stage) % 2
    for i in range(next_ref.shape[0]):
        mine, other = 2 * i + bit, 2 * i + 1 - bit
        send_ref[i] = (keep_ref[other] + recv_ref[other].astype(F32)).astype(BF16)
        next_ref[i] = keep_ref[mine] + recv_ref[mine].astype(F32)


def write_kernel(order, keep_ref, recv_ref, *refs):
    out_ref, sum_ref, sem = refs[-3:]
    odd = lax.axis_index("gx") % 2
    third = 1 if order is None else 2 * odd if order else 2 - 2 * odd
    width = sum_ref.shape[1]
    sum_ref[...] = keep_ref[0] + recv_ref[0].astype(F32)
    spot = pl.ds(pl.multiple_of(third * width, width), width)
    copy = pltpu.make_async_copy(sum_ref, out_ref.at[:, spot], sem)
    copy.start()
    copy.wait()


def gate_kernel(recv_ref, token_ref):
    token_ref[...] = jnp.zeros(token_ref.shape, F32)


def swapped(value, axis, step):
    length = lax.axis_size(axis)
    return lax.ppermute(value, axis, [(i, i ^ step) for i in range(length) if i ^ step < length])


def folded(keep, send, parts, after=()):
    left, share, width = keep.shape
    stage = 0
    while left > 1:
        recv = swapped(send, "gy", 1 << stage)
        stage += 1
        left //= 2
        keep, send = pl.pallas_call(
            functools.partial(fold_kernel, stage),
            out_shape=(
                jax.ShapeDtypeStruct((left, share, width), F32),
                jax.ShapeDtypeStruct((left, share, width), BF16),
            ),
            in_specs=[VMEM] * (2 + len(after)),
            out_specs=(VMEM, VMEM),
            compiler_params=PARAMS,
            name="fold",
        )(keep, recv, *after)
        after = ()
    return keep, swapped(send, "gy", 1 << stage), keep


def written(order, keep, recv, result):
    share, width = keep.shape[1:]
    start = order is None
    whole = jax.ShapeDtypeStruct((share, 3 * width), F32)
    return pl.pallas_call(
        functools.partial(write_kernel, order),
        out_shape=whole,
        in_specs=[VMEM, VMEM] if start else [VMEM, VMEM, HBM],
        out_specs=HBM,
        input_output_aliases={} if start else {2: 0},
        scratch_shapes=[pltpu.VMEM((share, width), F32), pltpu.SemaphoreType.DMA],
        compiler_params=PARAMS,
        cost_estimate=SHORT,
        name="write",
    )(keep, recv, *([] if start else [result]))


def body(a_blocks, a_cols, mushy, p_blocks, p_cols, send_rows):
    rows, size, inner = p_blocks.shape[1:]
    acol, pcol = a_cols.transpose(2, 0, 1), p_cols[0].T
    mush, sends = mushy[0], send_rows[0]
    ablk, pblk = a_blocks[0], p_blocks[0]
    count = sends.shape[0] // 2
    width = NCOL * size
    length = lax.axis_size("gx")
    parts = lax.axis_size("gy")
    share = width // parts

    tail = -(-count * pcol.shape[0] // 16) * 16
    packed = jax.ShapeDtypeStruct((count * size + tail, inner), BF16)

    first, second, info = pl.pallas_call(
        pack_kernel,
        out_shape=(packed, packed, jax.ShapeDtypeStruct((rows * INFO,), jnp.int32)),
        in_specs=[HBM] * 5,
        out_specs=(HBM, HBM, HBM),
        scratch_shapes=[
            pltpu.SMEM(sends.shape, sends.dtype),
            pltpu.SMEM(pcol.shape, pcol.dtype),
            pltpu.SMEM(acol.shape, acol.dtype),
            pltpu.SMEM(mush.shape, mush.dtype),
            pltpu.SMEM((rows * INFO,), jnp.int32),
            pltpu.VMEM(pblk.shape, BF16),
            pltpu.VMEM((2,) + packed.shape, BF16),
            pltpu.SemaphoreType.DMA((5,)),
        ],
        compiler_params=pltpu.CompilerParams(vmem_limit_bytes=56 * 1024 * 1024),
        cost_estimate=LONG,
        name="pack",
    )(sends, pcol, acol, mush, pblk)
    even = [(i, i + 1) for i in range(0, length - 1, 2)]
    uneven = [(i, i + 1) for i in range(1, length - 1, 2)]
    first = lax.ppermute(first, "gx", even + [(j, i) for i, j in even])
    split = jax.ShapeDtypeStruct((2, rows * size, count * size), BF16)
    high, low, second = pl.pallas_call(
        functools.partial(scatter_kernel, 1),
        out_shape=(split, split, packed),
        in_specs=[SMEM, VMEM, HBM],
        out_specs=(VMEM, VMEM, HBM),
        input_output_aliases={2: 2},
        compiler_params=PARAMS,
        cost_estimate=TINY,
        name="scatter",
    )(info, ablk, second)
    second = lax.ppermute(second, "gx", uneven + [(j, i) for i, j in uneven])

    partial = (
        jax.ShapeDtypeStruct((parts // 2, share, width), F32),
        jax.ShapeDtypeStruct((parts // 2, share, width), BF16),
    )
    own_t, keep, send = pl.pallas_call(
        functools.partial(own_kernel, parts),
        out_shape=(jax.ShapeDtypeStruct((width, rows * size), BF16),) + partial,
        in_specs=[SMEM, VMEM, VMEM],
        out_specs=(VMEM, VMEM, VMEM),
        scratch_shapes=[
            pltpu.VMEM((rows + 1, size, width), BF16),
            pltpu.VMEM((rows * size, width), BF16),
        ],
        compiler_params=PARAMS,
        cost_estimate=MEDIUM,
        name="own",
    )(info, ablk, pblk)
    keep, recv, folds = folded(keep, send, parts)
    high, low = pl.pallas_call(
        functools.partial(scatter_kernel, 0),
        out_shape=(split, split),
        in_specs=[SMEM, VMEM, VMEM, VMEM, VMEM],
        out_specs=(VMEM, VMEM),
        input_output_aliases={3: 0, 4: 1},
        compiler_params=PARAMS,
        cost_estimate=TINY,
        name="scatter",
    )(info, ablk, own_t, high, low)
    pieces = []
    for order, ghosts in enumerate((first, second)):
        after = [folds] if order else []
        pieces.append(
            pl.pallas_call(
                functools.partial(ghost_kernel, order),
                out_shape=partial,
                in_specs=[VMEM] * (4 + len(after)),
                out_specs=(VMEM, VMEM),
                scratch_shapes=[
                    pltpu.VMEM((count * size, width), BF16),
                    pltpu.VMEM((rows * size, width), BF16),
                ],
                compiler_params=PARAMS,
                cost_estimate=LONG,
                name="ghost",
            )(high, low, ghosts, own_t, *after)
        )
    token = pl.pallas_call(
        gate_kernel,
        out_shape=jax.ShapeDtypeStruct((8, LANES), F32),
        in_specs=[HBM],
        out_specs=VMEM,
        compiler_params=PARAMS,
        cost_estimate=LONG,
        name="gate",
    )(recv)
    sides = [folded(*pieces[0], parts), folded(*pieces[1], parts, (token,))]
    result = written(None, keep, recv, None)
    for order, (keep, recv, folds) in enumerate(sides):
        result = written(order, keep, recv, result)
    return result[None]


def solution(mesh):
    placed = (
        P("gx", "gy", None, None),
        P("gx", "gy", None),
        P("gx", "gy"),
        P("gx", "gy", None, None),
        P("gx", "gy", None),
        P("gx", "gy"),
    )
    return jax.shard_map(
        body, mesh=mesh, in_specs=placed, out_specs=P("gx", "gy", None), check_vma=False
    )
```

profile of v0, /device:TPU:24, one launch (start us, length us, event | category | flops | bytes accessed | tf_op | source)
XLA Modules:
  0.0 24.8 jit_solution(12319159903097972024)
XLA Ops:
  0.0 1.8 %pack.1 = (bf16[272,256]{1,0:T(8,128)(2,1)}, bf16[272,256]{1,0:T(8,128)(2,1)}, s32[1024]{0:T(1024)}) custom-call(s32[8]{0:T(128)} %bitcast.16, s32[4,8]{1,0:T(4,128)} %bitcast.15, s32[7,1,8]{2,1,0:T(1,128)} %bitcast.14, s32[8]{0:T(128)} %bitcast.17, bf16[8,64,256]{2,1,0:T(8,128)(2,1)} %bitcast.12), custom_call_target="tpu_custom_call" | custom-call | flops 10000000000 | bytes 1000000 | tf_op jit(solution)/shard_map/pack/pallas_call | solution.py:266
  1.8 1.6 %collective-permute-start.5 = (bf16[272,256]{1,0:T(8,128)(2,1)}, bf16[272,256]{1,0:T(8,128)(2,1)S(1)}, u32[]{:S(2)}, u32[]{:S(2)}) collective-permute-start(bf16[272,256]{1,0:T(8,128)(2,1)} %get-tuple-element.42), channel_id=1, source_target_pairs={{0,4},{8,12},{16,20},{24,28},{4,0},{12,8},{20,16},{28,24},{1,5},{9... | collective-permute-start | bytes 417800 | tf_op jit(solution)/shard_map/ppermute | solution.py:287
  3.4 0.6 %scatter.2 = (bf16[2,512,256]{2,1,0:T(8,128)(2,1)S(1)}, bf16[2,512,256]{2,1,0:T(8,128)(2,1)S(1)}, bf16[272,256]{1,0:T(8,128)(2,1)}) custom-call(s32[1024]{0:T(1024)S(1)} %copy-done.1, bf16[8,64,448]{2,1,0:T(8,128)(2,1)S(1)} %bitcast.9, bf16[272,256]{1,0:T(8,128)(2,1)} %get-tuple-element.28.passed), custom_call_target="tpu_custom_call", output_to_operand_aliasing={{2}: (2, {})} | custom-call | flops 1000000 | bytes 1000000 | tf_op jit(solution)/shard_map/scatter/pallas_call | solution.py:289
  4.0 3.2 %collective-permute-start = (bf16[272,256]{1,0:T(8,128)(2,1)}, bf16[272,256]{1,0:T(8,128)(2,1)S(1)}, u32[]{:S(2)}, u32[]{:S(2)}) collective-permute-start(bf16[272,256]{1,0:T(8,128)(2,1)} %get-tuple-element.33), channel_id=1, source_target_pairs={{4,8},{12,16},{20,24},{8,4},{16,12},{24,20},{5,9},{13,17},{21,25},... | collective-permute-start | bytes 417800 | tf_op jit(solution)/shard_map/ppermute | solution.py:299
  7.1 2.2 %own.1 = (bf16[512,512]{1,0:T(8,128)(2,1)S(1)}, f32[2,128,512]{2,1,0:T(8,128)S(1)}, bf16[2,128,512]{2,1,0:T(8,128)(2,1)S(1)}) custom-call(s32[1024]{0:T(1024)S(1)} %copy-done.1, bf16[8,64,448]{2,1,0:T(8,128)(2,1)S(1)} %bitcast.10, bf16[8,64,256]{2,1,0:T(8,128)(2,1)S(1)} %bitcast.13), custom_call_target="tpu_custom_call" | custom-call | flops 1000000000 | bytes 1000000 | tf_op jit(solution)/shard_map/own/pallas_call | solution.py:305
  9.4 0.1 collective-permute-start.1
  9.5 1.4 %scatter.3 = (bf16[2,512,256]{2,1,0:T(8,128)(2,1)S(1)}, bf16[2,512,256]{2,1,0:T(8,128)(2,1)S(1)}) custom-call(s32[1024]{0:T(1024)S(1)} %copy-done.1, bf16[8,64,448]{2,1,0:T(8,128)(2,1)S(1)} %bitcast.11, bf16[512,512]{1,0:T(8,128)(2,1)S(1)} %get-tuple-element.27.passed.ownt_ref, ...), custom_call_target="tpu_custom_call", output_to_operand_aliasing={{0}: (3, {}), {1}: (4, {})} | custom-call | flops 1000000 | bytes 1000000 | tf_op jit(solution)/shard_map/scatter/pallas_call | solution.py:319
  10.9 0.0 collective-permute-done.5.in_ref
  10.9 1.0 %ghost.3 = (f32[2,128,512]{2,1,0:T(8,128)S(1)}, bf16[2,128,512]{2,1,0:T(8,128)(2,1)S(1)}) custom-call(bf16[2,512,256]{2,1,0:T(8,128)(2,1)S(1)} %get-tuple-element.31.high_ref, bf16[2,512,256]{2,1,0:T(8,128)(2,1)S(1)} %get-tuple-element.32.low_ref, bf16[272,256]{1,0:T(8,128)(2,1)S(1)} %collective-permute-done.5.in_ref, ...), custom_call_target="tpu_custom_call" | custom-call | flops 10000000000 | bytes 1000000 | tf_op jit(solution)/shard_map/ghost/pallas_call | solution.py:333
  11.9 0.6 %collective-permute-start.6 = (bf16[2,128,512]{2,1,0:T(8,128)(2,1)S(1)}, bf16[2,128,512]{2,1,0:T(8,128)(2,1)S(1)}, u32[]{:S(2)}, u32[]{:S(2)}) collective-permute-start(bf16[2,128,512]{2,1,0:T(8,128)(2,1)S(1)} %get-tuple-element.44), channel_id=1, source_target_pairs={{0,1},{1,0},{2,3},{3,2},{4,5},{5,4},{6,7},{7,6},{8,9},{9,8},{10,11... | collective-permute-start | bytes 786440 | tf_op jit(solution)/shard_map/ppermute | solution.py:210
  12.5 0.0 collective-permute-done.1.recv_ref
  12.5 1.6 %collective-permute-start.3 = (bf16[1,128,512]{2,1,0:T(8,128)(2,1)S(1)}, bf16[1,128,512]{2,1,0:T(8,128)(2,1)S(1)}, u32[]{:S(2)}, u32[]{:S(2)}) collective-permute-start(bf16[1,128,512]{2,1,0:T(8,128)(2,1)S(1)} %get-tuple-element.39), channel_id=1, source_target_pairs={{0,2},{1,3},{2,0},{3,1},{4,6},{5,7},{6,4},{7,5},{8,10},{9,11},{10,... | collective-permute-start | bytes 393224 | tf_op jit(solution)/shard_map/ppermute | solution.py:210
  14.1 1.0 %ghost.2 = (f32[2,128,512]{2,1,0:T(8,128)S(1)}, bf16[2,128,512]{2,1,0:T(8,128)(2,1)S(1)}) custom-call(bf16[2,512,256]{2,1,0:T(8,128)(2,1)S(1)} %get-tuple-element.31.high_ref, bf16[2,512,256]{2,1,0:T(8,128)(2,1)S(1)} %get-tuple-element.32.low_ref, bf16[272,256]{1,0:T(8,128)(2,1)S(1)} %collective-permute-done.in_ref, ...), custom_call_target="tpu_custom_call" | custom-call | flops 10000000000 | bytes 1000000 | tf_op jit(solution)/shard_map/ghost/pallas_call | solution.py:333
  15.2 0.1 collective-permute-start.2
  15.3 0.1 fold.5
  15.4 0.6 %collective-permute-start.7 = (bf16[1,128,512]{2,1,0:T(8,128)(2,1)S(1)}, bf16[1,128,512]{2,1,0:T(8,128)(2,1)S(1)}, u32[]{:S(2)}, u32[]{:S(2)}) collective-permute-start(bf16[1,128,512]{2,1,0:T(8,128)(2,1)S(1)} %get-tuple-element.46), channel_id=1, source_target_pairs={{0,2},{1,3},{2,0},{3,1},{4,6},{5,7},{6,4},{7,5},{8,10},{9,11},{10,... | collective-permute-start | bytes 393224 | tf_op jit(solution)/shard_map/ppermute | solution.py:210
  15.9 2.1 %collective-permute-done.3.recv_ref = bf16[1,128,512]{2,1,0:T(8,128)(2,1)S(1)} collective-permute-done((bf16[1,128,512]{2,1,0:T(8,128)(2,1)S(1)}, bf16[1,128,512]{2,1,0:T(8,128)(2,1)S(1)}, u32[]{:S(2)}, u32[]{:S(2)}) %collective-permute-start.3) | collective-permute-done | bytes 131104 | tf_op jit(solution)/shard_map/ppermute | solution.py:210
  18.1 0.1 fold.4
  18.1 2.1 %collective-permute-start.4 = (bf16[1,128,512]{2,1,0:T(8,128)(2,1)S(1)}, bf16[1,128,512]{2,1,0:T(8,128)(2,1)S(1)}, u32[]{:S(2)}, u32[]{:S(2)}) collective-permute-start(bf16[1,128,512]{2,1,0:T(8,128)(2,1)S(1)} %get-tuple-element.41), channel_id=1, source_target_pairs={{0,2},{1,3},{2,0},{3,1},{4,6},{5,7},{6,4},{7,5},{8,10},{9,11},{10,... | collective-permute-start | bytes 393224 | tf_op jit(solution)/shard_map/ppermute | solution.py:210
  20.2 0.7 %write.3.refs_0_ = f32[128,1536]{1,0:T(8,128)} custom-call(f32[1,128,512]{2,1,0:T(8,128)S(1)} %get-tuple-element.36.refs_0_.keep_ref, bf16[1,128,512]{2,1,0:T(8,128)(2,1)S(1)} %collective-permute-done.3.recv_ref), custom_call_target="tpu_custom_call" | custom-call | flops 100000000 | bytes 1000000 | tf_op jit(solution)/shard_map/write/pallas_call | solution.py:239
  21.0 0.7 %collective-permute-done.7.recv_ref = bf16[1,128,512]{2,1,0:T(8,128)(2,1)S(1)} collective-permute-done((bf16[1,128,512]{2,1,0:T(8,128)(2,1)S(1)}, bf16[1,128,512]{2,1,0:T(8,128)(2,1)S(1)}, u32[]{:S(2)}, u32[]{:S(2)}) %collective-permute-start.7) | collective-permute-done | bytes 131104 | tf_op jit(solution)/shard_map/ppermute | solution.py:210
  21.7 0.7 %write.4.refs_0_ = f32[128,1536]{1,0:T(8,128)} custom-call(f32[1,128,512]{2,1,0:T(8,128)S(1)} %get-tuple-element.45.keep_ref, bf16[1,128,512]{2,1,0:T(8,128)(2,1)S(1)} %collective-permute-done.7.recv_ref, f32[128,1536]{1,0:T(8,128)} %write.3.refs_0_), custom_call_target="tpu_custom_call", output_to_operand_aliasing={{}: (2, {})} | custom-call | flops 100000000 | bytes 1000000 | tf_op jit(solution)/shard_map/write/pallas_call | solution.py:239
  22.5 1.6 %collective-permute-done.4.recv_ref = bf16[1,128,512]{2,1,0:T(8,128)(2,1)S(1)} collective-permute-done((bf16[1,128,512]{2,1,0:T(8,128)(2,1)S(1)}, bf16[1,128,512]{2,1,0:T(8,128)(2,1)S(1)}, u32[]{:S(2)}, u32[]{:S(2)}) %collective-permute-start.4) | collective-permute-done | bytes 131104 | tf_op jit(solution)/shard_map/ppermute | solution.py:210
  24.1 0.7 %write.5 = f32[128,1536]{1,0:T(8,128)} custom-call(f32[1,128,512]{2,1,0:T(8,128)S(1)} %get-tuple-element.40.keep_ref, bf16[1,128,512]{2,1,0:T(8,128)(2,1)S(1)} %collective-permute-done.4.recv_ref, f32[128,1536]{1,0:T(8,128)} %write.4.refs_0_), custom_call_target="tpu_custom_call", output_to_operand_aliasing={{}: (2, {})} | custom-call | flops 100000000 | bytes 1000000 | tf_op jit(solution)/shard_map/write/pallas_call | solution.py:239
  (11 shorter events, 0.1 us)
Async XLA Ops:
  0.0 3.3 %copy-start = (bf16[1,8,64,448]{3,2,1,0:T(8,128)(2,1)S(1)}, bf16[1,8,64,448]{3,2,1,0:T(8,128)(2,1)}, u32[]{:S(2)}) copy-start(bf16[1,8,64,448]{3,2,1,0:T(8,128)(2,1)} %param.6) | copy-start | bytes 1376260
  1.8 1.6 %copy-start.1 = (s32[1024]{0:T(1024)S(1)}, s32[1024]{0:T(1024)}, u32[]{:S(2)}) copy-start(s32[1024]{0:T(1024)} %get-tuple-element.26.info) | copy-start | bytes 12292
  1.8 9.1 %collective-permute-start.5 = (bf16[272,256]{1,0:T(8,128)(2,1)}, bf16[272,256]{1,0:T(8,128)(2,1)S(1)}, u32[]{:S(2)}, u32[]{:S(2)}) collective-permute-start(bf16[272,256]{1,0:T(8,128)(2,1)} %get-tuple-element.42), channel_id=1, source_target_pairs={{0,4},{8,12},{16,20},{24,28},{4,0},{12,8},{20,16},{28,24},{1,5},{9... | collective-permute-start | bytes 417800 | tf_op jit(solution)/shard_map/ppermute | solution.py:287
  3.4 3.8 %copy-start.2 = (bf16[1,8,64,256]{3,2,1,0:T(8,128)(2,1)S(1)}, bf16[1,8,64,256]{3,2,1,0:T(8,128)(2,1)}, u32[]{:S(2)}) copy-start(bf16[1,8,64,256]{3,2,1,0:T(8,128)(2,1)} %param.9) | copy-start | bytes 786436
  4.0 10.2 %collective-permute-start = (bf16[272,256]{1,0:T(8,128)(2,1)}, bf16[272,256]{1,0:T(8,128)(2,1)S(1)}, u32[]{:S(2)}, u32[]{:S(2)}) collective-permute-start(bf16[272,256]{1,0:T(8,128)(2,1)} %get-tuple-element.33), channel_id=1, source_target_pairs={{4,8},{12,16},{20,24},{8,4},{16,12},{24,20},{5,9},{13,17},{21,25},... | collective-permute-start | bytes 417800 | tf_op jit(solution)/shard_map/ppermute | solution.py:299
  9.4 3.1 %collective-permute-start.1 = (bf16[2,128,512]{2,1,0:T(8,128)(2,1)S(1)}, bf16[2,128,512]{2,1,0:T(8,128)(2,1)S(1)}, u32[]{:S(2)}, u32[]{:S(2)}) collective-permute-start(bf16[2,128,512]{2,1,0:T(8,128)(2,1)S(1)} %get-tuple-element.35), channel_id=1, source_target_pairs={{0,1},{1,0},{2,3},{3,2},{4,5},{5,4},{6,7},{7,6},{8,9},{9,8},{10,11... | collective-permute-start | bytes 786440 | tf_op jit(solution)/shard_map/ppermute | solution.py:210
  11.9 3.3 %collective-permute-start.6 = (bf16[2,128,512]{2,1,0:T(8,128)(2,1)S(1)}, bf16[2,128,512]{2,1,0:T(8,128)(2,1)S(1)}, u32[]{:S(2)}, u32[]{:S(2)}) collective-permute-start(bf16[2,128,512]{2,1,0:T(8,128)(2,1)S(1)} %get-tuple-element.44), channel_id=1, source_target_pairs={{0,1},{1,0},{2,3},{3,2},{4,5},{5,4},{6,7},{7,6},{8,9},{9,8},{10,11... | collective-permute-start | bytes 786440 | tf_op jit(solution)/shard_map/ppermute | solution.py:210
  12.5 5.5 %collective-permute-start.3 = (bf16[1,128,512]{2,1,0:T(8,128)(2,1)S(1)}, bf16[1,128,512]{2,1,0:T(8,128)(2,1)S(1)}, u32[]{:S(2)}, u32[]{:S(2)}) collective-permute-start(bf16[1,128,512]{2,1,0:T(8,128)(2,1)S(1)} %get-tuple-element.39), channel_id=1, source_target_pairs={{0,2},{1,3},{2,0},{3,1},{4,6},{5,7},{6,4},{7,5},{8,10},{9,11},{10,... | collective-permute-start | bytes 393224 | tf_op jit(solution)/shard_map/ppermute | solution.py:210
  15.2 2.9 %collective-permute-start.2 = (bf16[2,128,512]{2,1,0:T(8,128)(2,1)S(1)}, bf16[2,128,512]{2,1,0:T(8,128)(2,1)S(1)}, u32[]{:S(2)}, u32[]{:S(2)}) collective-permute-start(bf16[2,128,512]{2,1,0:T(8,128)(2,1)S(1)} %get-tuple-element.38), channel_id=1, source_target_pairs={{0,1},{1,0},{2,3},{3,2},{4,5},{5,4},{6,7},{7,6},{8,9},{9,8},{10,11... | collective-permute-start | bytes 786440 | tf_op jit(solution)/shard_map/ppermute | solution.py:210
  15.4 6.4 %collective-permute-start.7 = (bf16[1,128,512]{2,1,0:T(8,128)(2,1)S(1)}, bf16[1,128,512]{2,1,0:T(8,128)(2,1)S(1)}, u32[]{:S(2)}, u32[]{:S(2)}) collective-permute-start(bf16[1,128,512]{2,1,0:T(8,128)(2,1)S(1)} %get-tuple-element.46), channel_id=1, source_target_pairs={{0,2},{1,3},{2,0},{3,1},{4,6},{5,7},{6,4},{7,5},{8,10},{9,11},{10,... | collective-permute-start | bytes 393224 | tf_op jit(solution)/shard_map/ppermute | solution.py:210
  18.1 6.0 %collective-permute-start.4 = (bf16[1,128,512]{2,1,0:T(8,128)(2,1)S(1)}, bf16[1,128,512]{2,1,0:T(8,128)(2,1)S(1)}, u32[]{:S(2)}, u32[]{:S(2)}) collective-permute-start(bf16[1,128,512]{2,1,0:T(8,128)(2,1)S(1)} %get-tuple-element.41), channel_id=1, source_target_pairs={{0,2},{1,3},{2,0},{3,1},{4,6},{5,7},{6,4},{7,5},{8,10},{9,11},{10,... | collective-permute-start | bytes 393224 | tf_op jit(solution)/shard_map/ppermute | solution.py:210
where the time goes:
time: 25 us; the launch traced here: 24.8 us
  Pallas kernels  10.5 us (42%)
  starting transfers between devices  9.69 us (39%)
  waiting for transfers between devices  4.51 us (18%)
    ppermute x6, starting transfers between devices, swapped(): lax.ppermute(value, axis, [(i, i ^ step) for i in range(length) if i ^ st...  4.98 us
    ppermute x6, waiting for transfers between devices, swapped(): lax.ppermute(value, axis, [(i, i ^ step) for i in range(length) if i ^ st...  4.51 us
    ppermute x1, starting transfers between devices, body(): second = lax.ppermute(second, 'gx', uneven + [(j, i) for i, j in uneven])  3.15 us
    pallas_call x1, Pallas kernels, body(): pl.pallas_call(functools.partial(own_kernel, parts), out_shape=(jax.Shape...  2.25 us
    pallas_call x3, Pallas kernels, written(): pl.pallas_call(functools.partial(write_kernel, order), out_shape=whole, i...  2.22 us
    pallas_call x2, Pallas kernels, body(): pl.pallas_call(functools.partial(ghost_kernel, order), out_shape=partial,...  2.1 us
    pallas_call x1, Pallas kernels, body(): pl.pallas_call(pack_kernel, out_shape=(packed, packed, jax.ShapeDtypeStru...  1.77 us
    ppermute x1, starting transfers between devices, body(): first = lax.ppermute(first, 'gx', even + [(j, i) for i, j in even])  1.56 us
  transfers between devices with their start and end apart: 8, of which 3 were waited for; matrix products, arithmetic and copies ran while one was open for 0% of the time, Pallas kernels for 32%

commit v1 on v0

--- a/solution.py
+++ b/solution.py
@@ -9,7 +9,6 @@
 
 KA = 7
 KS = 3
-INFO = 128
 NCOL = 8
 LANES = 128
 WIDE = 256
@@ -38,11 +37,17 @@
     return tiles
 
 
-def masks_at(cols, size, dtype):
-    slots = (lax.broadcasted_iota(jnp.int32, (1, WIDE), 1) // size).astype(dtype)
+def masks_at(cols, size):
+    slots = (lax.broadcasted_iota(jnp.int32, (1, WIDE), 1) // size).astype(F32)
     return lambda first: [
         jnp.where(slots == col - first, 1.0, 0.0).astype(BF16) for col in cols
     ]
+
+
+def splats(info_ref, first, count, base):
+    info = info_ref[...].astype(F32) - base
+    shape = (info.shape[0], WIDE)
+    return [jnp.broadcast_to(info[:, first + k : first + k + 1], shape) for k in range(count)]
 
 
 def multiply(info, a_ref, base, ext_ref, prod_ref):
@@ -52,7 +57,7 @@
     for n in range(rows):
         picks = []
         for k in range(KA):
-            spot = info[n * INFO + k] - base
+            spot = info[n, k] - base
             good = (spot >= 0) & (spot < none)
             picks.append(jnp.where(good, spot, none))
         picked = jnp.concatenate([ext_ref[spot] for spot in picks], axis=0)
@@ -89,9 +94,9 @@
     for n in range(rows):
         limit = jnp.where(mush[n] > 0, KA, KS)
         for k in range(KA):
-            info[n * INFO + k] = jnp.where(k < limit, acol[k, 0, n], -1)
+            info[n, k] = jnp.where(k < limit, acol[k, 0, n], -1)
         for j in range(slots):
-            info[n * INFO + KA + j] = pcol[j, n]
+            info[n, KA + j] = pcol[j, n]
     passed = pltpu.make_async_copy(info, info_out, sems.at[0])
     passed.start()
     starts = ((1 - odd) * count, odd * count)
@@ -115,14 +120,16 @@
         copy.wait()
 
 
-def own_kernel(parts, info, a_ref, p_ref, ownt_ref, keep_ref, send_ref, own_ref, prod_ref):
+def own_kernel(parts, info_ref, a_ref, p_ref, ownt_ref, keep_ref, send_ref, own_ref, prod_ref, info, sem):
     bit = lax.axis_index("gy") % 2
     rows, size = p_ref.shape[0], p_ref.shape[1]
     width = NCOL * size
     share = width // parts
+    copy = pltpu.make_async_copy(info_ref, info, sem)
+    copy.start()
+    cols = splats(info_ref, KA, p_ref.shape[2] // size, 0)
     for n in range(rows):
-        cols = [info[n * INFO + KA + j] for j in range(p_ref.shape[2] // size)]
-        masks = masks_at(cols, size, jnp.int32)
+        masks = masks_at([col[n : n + 1, :] for col in cols], size)
         for c, tile in enumerate(spread(p_ref[n], masks, width)):
             own_ref[n, :, c * WIDE : (c + 1) * WIDE] = tile.astype(BF16)
     for c in range(width // LANES):
@@ -133,11 +140,12 @@
             spot = part // 2 + jnp.where(part % 2 == bit, 0, parts // 2)
             at = pl.ds(pl.multiple_of(spot * share, share), share)
             ownt_ref[at, :] = flipped[k * share : (k + 1) * share, :]
+    copy.wait()
     multiply(info, a_ref, 0, own_ref, prod_ref)
     finish(ownt_ref, prod_ref[...], keep_ref, send_ref)
 
 
-def scatter_kernel(when, info, a_ref, passed, *refs):
+def scatter_kernel(when, info_ref, a_ref, passed, *refs):
     high_ref, low_ref = refs[-3:-1] if when else refs[-2:]
     odd = lax.axis_index("gx") % 2
     rows, size = a_ref.shape[0], a_ref.shape[1]
@@ -145,12 +153,13 @@
 
     @pl.when(odd == when)
     def _():
-        for n in range(rows):
-            at = slice(n * size, (n + 1) * size)
-            for order in range(2):
-                right = odd if order else 1 - odd
-                base = rows + right * (width // size)
-                masks = masks_at([info[n * INFO + k] - base for k in range(KA)], size, jnp.int32)
+        for order in range(2):
+            right = odd if order else 1 - odd
+            base = rows + right * (width // size)
+            cols = splats(info_ref, 0, KA, base.astype(F32))
+            for n in range(rows):
+                at = slice(n * size, (n + 1) * size)
+                masks = masks_at([col[n : n + 1, :] for col in cols], size)
                 for c, tile in enumerate(spread(a_ref[n], masks, width)):
                     spot = slice(c * WIDE, (c + 1) * WIDE)
                     high = tile.astype(BF16)
@@ -167,7 +176,7 @@
     cols = in_ref[count * size :, :].astype(F32)
     for n in range(count):
         at = slice(n * size, (n + 1) * size)
-        masks = masks_at([cols[n * slots + j : n * slots + j + 1, :] for j in range(slots)], size, F32)
+        masks = masks_at([cols[n * slots + j : n * slots + j + 1, :] for j in range(slots)], size)
         for c, tile in enumerate(spread(in_ref[at, :], masks, width)):
             ext_ref[at, c * WIDE : (c + 1) * WIDE] = tile.astype(BF16)
     ext = ext_ref[...]
@@ -265,7 +274,7 @@
 
     first, second, info = pl.pallas_call(
         pack_kernel,
-        out_shape=(packed, packed, jax.ShapeDtypeStruct((rows * INFO,), jnp.int32)),
+        out_shape=(packed, packed, jax.ShapeDtypeStruct((rows, LANES), jnp.int32)),
         in_specs=[HBM] * 5,
         out_specs=(HBM, HBM, HBM),
         scratch_shapes=[
@@ -273,7 +282,7 @@
             pltpu.SMEM(pcol.shape, pcol.dtype),
             pltpu.SMEM(acol.shape, acol.dtype),
             pltpu.SMEM(mush.shape, mush.dtype),
-            pltpu.SMEM((rows * INFO,), jnp.int32),
+            pltpu.SMEM((rows, LANES), jnp.int32),
             pltpu.VMEM(pblk.shape, BF16),
             pltpu.VMEM((2,) + packed.shape, BF16),
             pltpu.SemaphoreType.DMA((5,)),
@@ -289,7 +298,7 @@
     high, low, second = pl.pallas_call(
         functools.partial(scatter_kernel, 1),
         out_shape=(split, split, packed),
-        in_specs=[SMEM, VMEM, HBM],
+        in_specs=[VMEM, VMEM, HBM],
         out_specs=(VMEM, VMEM, HBM),
         input_output_aliases={2: 2},
         compiler_params=PARAMS,
@@ -305,11 +314,13 @@
     own_t, keep, send = pl.pallas_call(
         functools.partial(own_kernel, parts),
         out_shape=(jax.ShapeDtypeStruct((width, rows * size), BF16),) + partial,
-        in_specs=[SMEM, VMEM, VMEM],
+        in_specs=[VMEM, VMEM, VMEM],
         out_specs=(VMEM, VMEM, VMEM),
         scratch_shapes=[
             pltpu.VMEM((rows + 1, size, width), BF16),
             pltpu.VMEM((rows * size, width), BF16),
+            pltpu.SMEM((rows, LANES), jnp.int32),
+            pltpu.SemaphoreType.DMA,
         ],
         compiler_params=PARAMS,
         cost_estimate=MEDIUM,
@@ -319,7 +330,7 @@
     high, low = pl.pallas_call(
         functools.partial(scatter_kernel, 0),
         out_shape=(split, split),
-        in_specs=[SMEM, VMEM, VMEM, VMEM, VMEM],
+        in_specs=[VMEM, VMEM, VMEM, VMEM, VMEM],
         out_specs=(VMEM, VMEM),
         input_output_aliases={3: 0, 4: 1},
         compiler_params=PARAMS,

time: 25 us -> 23.8 us (0.952)
  Pallas kernels: 10.5 us -> 9.28 us
    pallas_call x1, Pallas kernels: 0.62 us -> 0.01 us  [body(): pl.pallas_call(functools.partial(scatter_kernel, 1), out_shape=(split, sp...]
    pallas_call x1, Pallas kernels: 1.38 us -> 0.86 us  [body(): pl.pallas_call(functools.partial(scatter_kernel, 0), out_shape=(split, sp...]
  transfers between devices with their start and end apart: 8 -> 8, of which waited for: 3 -> 3; matrix products, arithmetic and copies ran while one was open for 0% -> 0% of each run, Pallas kernels for 32% -> 29%
where the time goes in v1:
time: 23.8 us; the launch traced here: 23.7 us
  starting transfers between devices  9.76 us (41%)
  Pallas kernels  9.28 us (39%)
  waiting for transfers between devices  4.51 us (19%)
    ppermute x6, starting transfers between devices, swapped(): lax.ppermute(value, axis, [(i, i ^ step) for i in range(length) if i ^ st...  4.97 us
    ppermute x6, waiting for transfers between devices, swapped(): lax.ppermute(value, axis, [(i, i ^ step) for i in range(length) if i ^ st...  4.51 us
    ppermute x1, starting transfers between devices, body(): second = lax.ppermute(second, 'gx', uneven + [(j, i) for i, j in uneven])  3.24 us
    pallas_call x3, Pallas kernels, written(): pl.pallas_call(functools.partial(write_kernel, order), out_shape=whole, i...  2.22 us
    pallas_call x1, Pallas kernels, body(): pl.pallas_call(functools.partial(own_kernel, parts), out_shape=(jax.Shape...  2.17 us
    pallas_call x2, Pallas kernels, body(): pl.pallas_call(functools.partial(ghost_kernel, order), out_shape=partial,...  2.1 us
    pallas_call x1, Pallas kernels, body(): pl.pallas_call(pack_kernel, out_shape=(packed, packed, jax.ShapeDtypeStru...  1.77 us
    ppermute x1, starting transfers between devices, body(): first = lax.ppermute(first, 'gx', even + [(j, i) for i, j in even])  1.56 us
  transfers between devices with their start and end apart: 8, of which 3 were waited for; matrix products, arithmetic and copies ran while one was open for 0% of the time, Pallas kernels for 29%

profile of v1, /device:TPU:24, one launch (start us, length us, event | category | flops | bytes accessed | tf_op | source)
XLA Modules:
  0.0 23.7 jit_solution(7764975077591416758)
XLA Ops:
  0.0 1.8 %pack.1 = (bf16[272,256]{1,0:T(8,128)(2,1)}, bf16[272,256]{1,0:T(8,128)(2,1)}, s32[8,128]{1,0:T(8,128)}) custom-call(s32[8]{0:T(128)} %bitcast.16, s32[4,8]{1,0:T(4,128)} %bitcast.15, s32[7,1,8]{2,1,0:T(1,128)} %bitcast.14, s32[8]{0:T(128)} %bitcast.17, bf16[8,64,256]{2,1,0:T(8,128)(2,1)} %bitcast.12), custom_call_target="tpu_custom_call" | custom-call | flops 10000000000 | bytes 1000000 | tf_op jit(solution)/shard_map/pack/pallas_call | solution.py:275
  1.8 1.6 %collective-permute-start.5 = (bf16[272,256]{1,0:T(8,128)(2,1)}, bf16[272,256]{1,0:T(8,128)(2,1)S(1)}, u32[]{:S(2)}, u32[]{:S(2)}) collective-permute-start(bf16[272,256]{1,0:T(8,128)(2,1)} %get-tuple-element.42), channel_id=1, source_target_pairs={{0,4},{8,12},{16,20},{24,28},{4,0},{12,8},{20,16},{28,24},{1,5},{9... | collective-permute-start | bytes 417800 | tf_op jit(solution)/shard_map/ppermute | solution.py:296
  3.4 3.2 %collective-permute-start = (bf16[272,256]{1,0:T(8,128)(2,1)}, bf16[272,256]{1,0:T(8,128)(2,1)S(1)}, u32[]{:S(2)}, u32[]{:S(2)}) collective-permute-start(bf16[272,256]{1,0:T(8,128)(2,1)} %get-tuple-element.33), channel_id=1, source_target_pairs={{4,8},{12,16},{20,24},{8,4},{16,12},{24,20},{5,9},{13,17},{21,25},... | collective-permute-start | bytes 417800 | tf_op jit(solution)/shard_map/ppermute | solution.py:308
  6.6 2.2 %own.1 = (bf16[512,512]{1,0:T(8,128)(2,1)S(1)}, f32[2,128,512]{2,1,0:T(8,128)S(1)}, bf16[2,128,512]{2,1,0:T(8,128)(2,1)S(1)}) custom-call(s32[8,128]{1,0:T(8,128)S(1)} %copy-done.1, bf16[8,64,448]{2,1,0:T(8,128)(2,1)S(1)} %bitcast.10, bf16[8,64,256]{2,1,0:T(8,128)(2,1)S(1)} %bitcast.13), custom_call_target="tpu_custom_call" | custom-call | flops 1000000000 | bytes 1000000 | tf_op jit(solution)/shard_map/own/pallas_call | solution.py:314
  8.8 0.1 collective-permute-start.1
  8.9 0.9 %scatter.3 = (bf16[2,512,256]{2,1,0:T(8,128)(2,1)S(1)}, bf16[2,512,256]{2,1,0:T(8,128)(2,1)S(1)}) custom-call(s32[8,128]{1,0:T(8,128)S(1)} %copy-done.1, bf16[8,64,448]{2,1,0:T(8,128)(2,1)S(1)} %bitcast.11, bf16[512,512]{1,0:T(8,128)(2,1)S(1)} %get-tuple-element.27.passed.ownt_ref, ...), custom_call_target="tpu_custom_call", output_to_operand_aliasing={{0}: (3, {}), {1}: (4, {})} | custom-call | flops 1000000 | bytes 1000000 | tf_op jit(solution)/shard_map/scatter/pallas_call | solution.py:330
  9.7 1.0 %ghost.3 = (f32[2,128,512]{2,1,0:T(8,128)S(1)}, bf16[2,128,512]{2,1,0:T(8,128)(2,1)S(1)}) custom-call(bf16[2,512,256]{2,1,0:T(8,128)(2,1)S(1)} %get-tuple-element.31.high_ref, bf16[2,512,256]{2,1,0:T(8,128)(2,1)S(1)} %get-tuple-element.32.low_ref, bf16[272,256]{1,0:T(8,128)(2,1)S(1)} %collective-permute-done.5.in_ref, ...), custom_call_target="tpu_custom_call" | custom-call | flops 10000000000 | bytes 1000000 | tf_op jit(solution)/shard_map/ghost/pallas_call | solution.py:344
  10.8 0.5 %collective-permute-start.6 = (bf16[2,128,512]{2,1,0:T(8,128)(2,1)S(1)}, bf16[2,128,512]{2,1,0:T(8,128)(2,1)S(1)}, u32[]{:S(2)}, u32[]{:S(2)}) collective-permute-start(bf16[2,128,512]{2,1,0:T(8,128)(2,1)S(1)} %get-tuple-element.44), channel_id=1, source_target_pairs={{0,1},{1,0},{2,3},{3,2},{4,5},{5,4},{6,7},{7,6},{8,9},{9,8},{10,11... | collective-permute-start | bytes 786440 | tf_op jit(solution)/shard_map/ppermute | solution.py:219
  11.3 0.0 collective-permute-done.1.recv_ref
  11.4 1.6 %collective-permute-start.3 = (bf16[1,128,512]{2,1,0:T(8,128)(2,1)S(1)}, bf16[1,128,512]{2,1,0:T(8,128)(2,1)S(1)}, u32[]{:S(2)}, u32[]{:S(2)}) collective-permute-start(bf16[1,128,512]{2,1,0:T(8,128)(2,1)S(1)} %get-tuple-element.39), channel_id=1, source_target_pairs={{0,2},{1,3},{2,0},{3,1},{4,6},{5,7},{6,4},{7,5},{8,10},{9,11},{10,... | collective-permute-start | bytes 393224 | tf_op jit(solution)/shard_map/ppermute | solution.py:219
  13.0 1.0 %ghost.2 = (f32[2,128,512]{2,1,0:T(8,128)S(1)}, bf16[2,128,512]{2,1,0:T(8,128)(2,1)S(1)}) custom-call(bf16[2,512,256]{2,1,0:T(8,128)(2,1)S(1)} %get-tuple-element.31.high_ref, bf16[2,512,256]{2,1,0:T(8,128)(2,1)S(1)} %get-tuple-element.32.low_ref, bf16[272,256]{1,0:T(8,128)(2,1)S(1)} %collective-permute-done.in_ref, ...), custom_call_target="tpu_custom_call" | custom-call | flops 10000000000 | bytes 1000000 | tf_op jit(solution)/shard_map/ghost/pallas_call | solution.py:344
  14.0 0.1 collective-permute-start.2
  14.1 0.0 collective-permute-done.6.recv_ref
  14.1 0.1 fold.5
  14.2 0.6 %collective-permute-start.7 = (bf16[1,128,512]{2,1,0:T(8,128)(2,1)S(1)}, bf16[1,128,512]{2,1,0:T(8,128)(2,1)S(1)}, u32[]{:S(2)}, u32[]{:S(2)}) collective-permute-start(bf16[1,128,512]{2,1,0:T(8,128)(2,1)S(1)} %get-tuple-element.46), channel_id=1, source_target_pairs={{0,2},{1,3},{2,0},{3,1},{4,6},{5,7},{6,4},{7,5},{8,10},{9,11},{10,... | collective-permute-start | bytes 393224 | tf_op jit(solution)/shard_map/ppermute | solution.py:219
  14.8 2.1 %collective-permute-done.3.recv_ref = bf16[1,128,512]{2,1,0:T(8,128)(2,1)S(1)} collective-permute-done((bf16[1,128,512]{2,1,0:T(8,128)(2,1)S(1)}, bf16[1,128,512]{2,1,0:T(8,128)(2,1)S(1)}, u32[]{:S(2)}, u32[]{:S(2)}) %collective-permute-start.3) | collective-permute-done | bytes 131104 | tf_op jit(solution)/shard_map/ppermute | solution.py:219
  16.9 0.0 collective-permute-done.2.recv_ref
  16.9 0.1 fold.4
  17.0 2.1 %collective-permute-start.4 = (bf16[1,128,512]{2,1,0:T(8,128)(2,1)S(1)}, bf16[1,128,512]{2,1,0:T(8,128)(2,1)S(1)}, u32[]{:S(2)}, u32[]{:S(2)}) collective-permute-start(bf16[1,128,512]{2,1,0:T(8,128)(2,1)S(1)} %get-tuple-element.41), channel_id=1, source_target_pairs={{0,2},{1,3},{2,0},{3,1},{4,6},{5,7},{6,4},{7,5},{8,10},{9,11},{10,... | collective-permute-start | bytes 393224 | tf_op jit(solution)/shard_map/ppermute | solution.py:219
  19.1 0.7 %write.3.refs_0_ = f32[128,1536]{1,0:T(8,128)} custom-call(f32[1,128,512]{2,1,0:T(8,128)S(1)} %get-tuple-element.36.refs_0_.keep_ref, bf16[1,128,512]{2,1,0:T(8,128)(2,1)S(1)} %collective-permute-done.3.recv_ref), custom_call_target="tpu_custom_call" | custom-call | flops 100000000 | bytes 1000000 | tf_op jit(solution)/shard_map/write/pallas_call | solution.py:248
  19.8 0.7 %collective-permute-done.7.recv_ref = bf16[1,128,512]{2,1,0:T(8,128)(2,1)S(1)} collective-permute-done((bf16[1,128,512]{2,1,0:T(8,128)(2,1)S(1)}, bf16[1,128,512]{2,1,0:T(8,128)(2,1)S(1)}, u32[]{:S(2)}, u32[]{:S(2)}) %collective-permute-start.7) | collective-permute-done | bytes 131104 | tf_op jit(solution)/shard_map/ppermute | solution.py:219
  20.6 0.7 %write.4.refs_0_ = f32[128,1536]{1,0:T(8,128)} custom-call(f32[1,128,512]{2,1,0:T(8,128)S(1)} %get-tuple-element.45.keep_ref, bf16[1,128,512]{2,1,0:T(8,128)(2,1)S(1)} %collective-permute-done.7.recv_ref, f32[128,1536]{1,0:T(8,128)} %write.3.refs_0_), custom_call_target="tpu_custom_call", output_to_operand_aliasing={{}: (2, {})} | custom-call | flops 100000000 | bytes 1000000 | tf_op jit(solution)/shard_map/write/pallas_call | solution.py:248
  21.3 1.6 %collective-permute-done.4.recv_ref = bf16[1,128,512]{2,1,0:T(8,128)(2,1)S(1)} collective-permute-done((bf16[1,128,512]{2,1,0:T(8,128)(2,1)S(1)}, bf16[1,128,512]{2,1,0:T(8,128)(2,1)S(1)}, u32[]{:S(2)}, u32[]{:S(2)}) %collective-permute-start.4) | collective-permute-done | bytes 131104 | tf_op jit(solution)/shard_map/ppermute | solution.py:219
  23.0 0.7 %write.5 = f32[128,1536]{1,0:T(8,128)} custom-call(f32[1,128,512]{2,1,0:T(8,128)S(1)} %get-tuple-element.40.keep_ref, bf16[1,128,512]{2,1,0:T(8,128)(2,1)S(1)} %collective-permute-done.4.recv_ref, f32[128,1536]{1,0:T(8,128)} %write.4.refs_0_), custom_call_target="tpu_custom_call", output_to_operand_aliasing={{}: (2, {})} | custom-call | flops 100000000 | bytes 1000000 | tf_op jit(solution)/shard_map/write/pallas_call | solution.py:248
  (11 shorter events, 0.1 us)
Async XLA Ops:
  0.0 3.3 %copy-start = (bf16[1,8,64,448]{3,2,1,0:T(8,128)(2,1)S(1)}, bf16[1,8,64,448]{3,2,1,0:T(8,128)(2,1)}, u32[]{:S(2)}) copy-start(bf16[1,8,64,448]{3,2,1,0:T(8,128)(2,1)} %param.6) | copy-start | bytes 1376260
  1.8 1.6 %copy-start.1 = (s32[8,128]{1,0:T(8,128)S(1)}, s32[8,128]{1,0:T(8,128)}, u32[]{:S(2)}) copy-start(s32[8,128]{1,0:T(8,128)} %get-tuple-element.26.info_ref) | copy-start | bytes 12292
  1.8 7.9 %collective-permute-start.5 = (bf16[272,256]{1,0:T(8,128)(2,1)}, bf16[272,256]{1,0:T(8,128)(2,1)S(1)}, u32[]{:S(2)}, u32[]{:S(2)}) collective-permute-start(bf16[272,256]{1,0:T(8,128)(2,1)} %get-tuple-element.42), channel_id=1, source_target_pairs={{0,4},{8,12},{16,20},{24,28},{4,0},{12,8},{20,16},{28,24},{1,5},{9... | collective-permute-start | bytes 417800 | tf_op jit(solution)/shard_map/ppermute | solution.py:296
  3.4 3.3 %copy-start.2 = (bf16[1,8,64,256]{3,2,1,0:T(8,128)(2,1)S(1)}, bf16[1,8,64,256]{3,2,1,0:T(8,128)(2,1)}, u32[]{:S(2)}) copy-start(bf16[1,8,64,256]{3,2,1,0:T(8,128)(2,1)} %param.9) | copy-start | bytes 786436
  3.4 9.6 %collective-permute-start = (bf16[272,256]{1,0:T(8,128)(2,1)}, bf16[272,256]{1,0:T(8,128)(2,1)S(1)}, u32[]{:S(2)}, u32[]{:S(2)}) collective-permute-start(bf16[272,256]{1,0:T(8,128)(2,1)} %get-tuple-element.33), channel_id=1, source_target_pairs={{4,8},{12,16},{20,24},{8,4},{16,12},{24,20},{5,9},{13,17},{21,25},... | collective-permute-start | bytes 417800 | tf_op jit(solution)/shard_map/ppermute | solution.py:308
  8.8 2.6 %collective-permute-start.1 = (bf16[2,128,512]{2,1,0:T(8,128)(2,1)S(1)}, bf16[2,128,512]{2,1,0:T(8,128)(2,1)S(1)}, u32[]{:S(2)}, u32[]{:S(2)}) collective-permute-start(bf16[2,128,512]{2,1,0:T(8,128)(2,1)S(1)} %get-tuple-element.35), channel_id=1, source_target_pairs={{0,1},{1,0},{2,3},{3,2},{4,5},{5,4},{6,7},{7,6},{8,9},{9,8},{10,11... | collective-permute-start | bytes 786440 | tf_op jit(solution)/shard_map/ppermute | solution.py:219
  10.8 3.3 %collective-permute-start.6 = (bf16[2,128,512]{2,1,0:T(8,128)(2,1)S(1)}, bf16[2,128,512]{2,1,0:T(8,128)(2,1)S(1)}, u32[]{:S(2)}, u32[]{:S(2)}) collective-permute-start(bf16[2,128,512]{2,1,0:T(8,128)(2,1)S(1)} %get-tuple-element.44), channel_id=1, source_target_pairs={{0,1},{1,0},{2,3},{3,2},{4,5},{5,4},{6,7},{7,6},{8,9},{9,8},{10,11... | collective-permute-start | bytes 786440 | tf_op jit(solution)/shard_map/ppermute | solution.py:219
  11.4 5.5 %collective-permute-start.3 = (bf16[1,128,512]{2,1,0:T(8,128)(2,1)S(1)}, bf16[1,128,512]{2,1,0:T(8,128)(2,1)S(1)}, u32[]{:S(2)}, u32[]{:S(2)}) collective-permute-start(bf16[1,128,512]{2,1,0:T(8,128)(2,1)S(1)} %get-tuple-element.39), channel_id=1, source_target_pairs={{0,2},{1,3},{2,0},{3,1},{4,6},{5,7},{6,4},{7,5},{8,10},{9,11},{10,... | collective-permute-start | bytes 393224 | tf_op jit(solution)/shard_map/ppermute | solution.py:219
  14.0 2.9 %collective-permute-start.2 = (bf16[2,128,512]{2,1,0:T(8,128)(2,1)S(1)}, bf16[2,128,512]{2,1,0:T(8,128)(2,1)S(1)}, u32[]{:S(2)}, u32[]{:S(2)}) collective-permute-start(bf16[2,128,512]{2,1,0:T(8,128)(2,1)S(1)} %get-tuple-element.38), channel_id=1, source_target_pairs={{0,1},{1,0},{2,3},{3,2},{4,5},{5,4},{6,7},{7,6},{8,9},{9,8},{10,11... | collective-permute-start | bytes 786440 | tf_op jit(solution)/shard_map/ppermute | solution.py:219
  14.2 6.4 %collective-permute-start.7 = (bf16[1,128,512]{2,1,0:T(8,128)(2,1)S(1)}, bf16[1,128,512]{2,1,0:T(8,128)(2,1)S(1)}, u32[]{:S(2)}, u32[]{:S(2)}) collective-permute-start(bf16[1,128,512]{2,1,0:T(8,128)(2,1)S(1)} %get-tuple-element.46), channel_id=1, source_target_pairs={{0,2},{1,3},{2,0},{3,1},{4,6},{5,7},{6,4},{7,5},{8,10},{9,11},{10,... | collective-permute-start | bytes 393224 | tf_op jit(solution)/shard_map/ppermute | solution.py:219
  17.0 6.0 %collective-permute-start.4 = (bf16[1,128,512]{2,1,0:T(8,128)(2,1)S(1)}, bf16[1,128,512]{2,1,0:T(8,128)(2,1)S(1)}, u32[]{:S(2)}, u32[]{:S(2)}) collective-permute-start(bf16[1,128,512]{2,1,0:T(8,128)(2,1)S(1)} %get-tuple-element.41), channel_id=1, source_target_pairs={{0,2},{1,3},{2,0},{3,1},{4,6},{5,7},{6,4},{7,5},{8,10},{9,11},{10,... | collective-permute-start | bytes 393224 | tf_op jit(solution)/shard_map/ppermute | solution.py:219

commit v2 on v1

--- a/solution.py
+++ b/solution.py
@@ -132,6 +132,8 @@
         masks = masks_at([col[n : n + 1, :] for col in cols], size)
         for c, tile in enumerate(spread(p_ref[n], masks, width)):
             own_ref[n, :, c * WIDE : (c + 1) * WIDE] = tile.astype(BF16)
+    copy.wait()
+    multiply(info, a_ref, 0, own_ref, prod_ref)
     for c in range(width // LANES):
         column = own_ref[:rows, :, c * LANES : (c + 1) * LANES]
         flipped = column.reshape(rows * size, LANES).T
@@ -140,35 +142,40 @@
             spot = part // 2 + jnp.where(part % 2 == bit, 0, parts // 2)
             at = pl.ds(pl.multiple_of(spot * share, share), share)
             ownt_ref[at, :] = flipped[k * share : (k + 1) * share, :]
-    copy.wait()
-    multiply(info, a_ref, 0, own_ref, prod_ref)
     finish(ownt_ref, prod_ref[...], keep_ref, send_ref)
+
+
+def scatter(order, info_ref, a_ref, high_ref, low_ref):
+    odd = lax.axis_index("gx") % 2
+    right = odd if order else 1 - odd
+    rows, size = a_ref.shape[0], a_ref.shape[1]
+    width = high_ref.shape[1]
+    base = rows + right * (width // size)
+    cols = splats(info_ref, 0, KA, base.astype(F32))
+    for n in range(rows):
+        at = slice(n * size, (n + 1) * size)
+        masks = masks_at([col[n : n + 1, :] for col in cols], size)
+        for c, tile in enumerate(spread(a_ref[n], masks, width)):
+            spot = slice(c * WIDE, (c + 1) * WIDE)
+            high = tile.astype(BF16)
+            high_ref[at, spot] = high
+            low_ref[at, spot] = (tile - high.astype(F32)).astype(BF16)
 
 
 def scatter_kernel(when, info_ref, a_ref, passed, *refs):
     high_ref, low_ref = refs[-3:-1] if when else refs[-2:]
-    odd = lax.axis_index("gx") % 2
-    rows, size = a_ref.shape[0], a_ref.shape[1]
-    width = high_ref.shape[2]
-
-    @pl.when(odd == when)
+
+    @pl.when(lax.axis_index("gx") % 2 == when)
     def _():
-        for order in range(2):
-            right = odd if order else 1 - odd
-            base = rows + right * (width // size)
-            cols = splats(info_ref, 0, KA, base.astype(F32))
-            for n in range(rows):
-                at = slice(n * size, (n + 1) * size)
-                masks = masks_at([col[n : n + 1, :] for col in cols], size)
-                for c, tile in enumerate(spread(a_ref[n], masks, width)):
-                    spot = slice(c * WIDE, (c + 1) * WIDE)
-                    high = tile.astype(BF16)
-                    high_ref[order, at, spot] = high
-                    low_ref[order, at, spot] = (tile - high.astype(F32)).astype(BF16)
+        for order in range(1 + when):
+            scatter(order, info_ref, a_ref, high_ref.at[order], low_ref.at[order])
 
 
 def ghost_kernel(order, high_ref, low_ref, in_ref, ownt_ref, *refs):
-    keep_ref, send_ref, ext_ref, prod_ref = refs[-4:]
+    if order:
+        info_ref, a_ref, after, keep_ref, send_ref, ext_ref, prod_ref, mine_high, mine_low = refs
+    else:
+        keep_ref, send_ref, ext_ref, prod_ref = refs
     width = ownt_ref.shape[0]
     size = width // NCOL
     slots = in_ref.shape[1] // size
@@ -179,13 +186,30 @@
         masks = masks_at([cols[n * slots + j : n * slots + j + 1, :] for j in range(slots)], size)
         for c, tile in enumerate(spread(in_ref[at, :], masks, width)):
             ext_ref[at, c * WIDE : (c + 1) * WIDE] = tile.astype(BF16)
-    ext = ext_ref[...]
-    step = prod_ref.shape[0] // 2
-    for m in range(2):
-        at = slice(m * step, (m + 1) * step)
-        value = jnp.dot(high_ref[order, at, :], ext, preferred_element_type=F32)
-        value += jnp.dot(low_ref[order, at, :], ext, preferred_element_type=F32)
-        prod_ref[at, :] = value.astype(BF16)
+
+    def product(high, low):
+        ext = ext_ref[...]
+        step = prod_ref.shape[0] // 2
+        for m in range(2):
+            at = slice(m * step, (m + 1) * step)
+            value = jnp.dot(high[at, :], ext, preferred_element_type=F32)
+            value += jnp.dot(low[at, :], ext, preferred_element_type=F32)
+            prod_ref[at, :] = value.astype(BF16)
+
+    if order:
+        odd = lax.axis_index("gx") % 2
+
+        @pl.when(odd == 0)
+        def _():
+            scatter(1, info_ref, a_ref, mine_high, mine_low)
+            product(mine_high, mine_low)
+
+        @pl.when(odd == 1)
+        def _():
+            product(high_ref.at[1], low_ref.at[1])
+
+    else:
+        product(high_ref.at[0], low_ref.at[0])
     finish(ownt_ref, prod_ref[...], keep_ref, send_ref)
 
 
@@ -339,21 +363,22 @@
     )(info, ablk, own_t, high, low)
     pieces = []
     for order, ghosts in enumerate((first, second)):
-        after = [folds] if order else []
+        more = [info, ablk, folds] if order else []
         pieces.append(
             pl.pallas_call(
                 functools.partial(ghost_kernel, order),
                 out_shape=partial,
-                in_specs=[VMEM] * (4 + len(after)),
+                in_specs=[VMEM] * (4 + len(more)),
                 out_specs=(VMEM, VMEM),
                 scratch_shapes=[
                     pltpu.VMEM((count * size, width), BF16),
                     pltpu.VMEM((rows * size, width), BF16),
-                ],
+                ]
+                + [pltpu.VMEM((rows * size, count * size), BF16)] * (2 * order),
                 compiler_params=PARAMS,
                 cost_estimate=LONG,
                 name="ghost",
-            )(high, low, ghosts, own_t, *after)
+            )(high, low, ghosts, own_t, *more)
         )
     token = pl.pallas_call(
         gate_kernel,

time: 23.8 us -> 23.6 us (level)
    pallas_call x2, Pallas kernels: 2.1 us -> 2.62 us  [body(): pl.pallas_call(functools.partial(ghost_kernel, order), out_shape=partial,...]
    pallas_call x1, Pallas kernels: 2.17 us -> 1.73 us  [body(): pl.pallas_call(functools.partial(own_kernel, parts), out_shape=(jax.Shape...]
    pallas_call x1, Pallas kernels: 0.86 us -> 0.53 us  [body(): pl.pallas_call(functools.partial(scatter_kernel, 0), out_shape=(split, sp...]
  transfers between devices with their start and end apart: 8 -> 8, of which waited for: 3 -> 3; matrix products, arithmetic and copies ran while one was open for 0% -> 0% of each run, Pallas kernels for 29% -> 28%
where the time goes in v2:
time: 23.6 us; the launch traced here: 23.5 us
  starting transfers between devices  9.64 us (41%)
  Pallas kernels  9.05 us (38%)
  waiting for transfers between devices  4.63 us (20%)
    ppermute x6, starting transfers between devices, swapped(): lax.ppermute(value, axis, [(i, i ^ step) for i in range(length) if i ^ st...  4.85 us
    ppermute x6, waiting for transfers between devices, swapped(): lax.ppermute(value, axis, [(i, i ^ step) for i in range(length) if i ^ st...  4.63 us
    ppermute x1, starting transfers between devices, body(): second = lax.ppermute(second, 'gx', uneven + [(j, i) for i, j in uneven])  3.24 us
    pallas_call x2, Pallas kernels, body(): pl.pallas_call(functools.partial(ghost_kernel, order), out_shape=partial,...  2.62 us
    pallas_call x3, Pallas kernels, written(): pl.pallas_call(functools.partial(write_kernel, order), out_shape=whole, i...  2.22 us
    pallas_call x1, Pallas kernels, body(): pl.pallas_call(pack_kernel, out_shape=(packed, packed, jax.ShapeDtypeStru...  1.77 us
    pallas_call x1, Pallas kernels, body(): pl.pallas_call(functools.partial(own_kernel, parts), out_shape=(jax.Shape...  1.73 us
    ppermute x1, starting transfers between devices, body(): first = lax.ppermute(first, 'gx', even + [(j, i) for i, j in even])  1.56 us
  transfers between devices with their start and end apart: 8, of which 3 were waited for; matrix products, arithmetic and copies ran while one was open for 0% of the time, Pallas kernels for 28%

profile of v2, /device:TPU:24, one launch (start us, length us, event | category | flops | bytes accessed | tf_op | source)
XLA Modules:
  0.0 23.5 jit_solution(6249751090748758527)
XLA Ops:
  0.0 1.8 %pack.1 = (bf16[272,256]{1,0:T(8,128)(2,1)}, bf16[272,256]{1,0:T(8,128)(2,1)}, s32[8,128]{1,0:T(8,128)}) custom-call(s32[8]{0:T(128)} %bitcast.17, s32[4,8]{1,0:T(4,128)} %bitcast.16, s32[7,1,8]{2,1,0:T(1,128)} %bitcast.15, s32[8]{0:T(128)} %bitcast.18, bf16[8,64,256]{2,1,0:T(8,128)(2,1)} %bitcast.13), custom_call_target="tpu_custom_call" | custom-call | flops 10000000000 | bytes 1000000 | tf_op jit(solution)/shard_map/pack/pallas_call | solution.py:299
  1.8 1.6 %collective-permute-start.5 = (bf16[272,256]{1,0:T(8,128)(2,1)}, bf16[272,256]{1,0:T(8,128)(2,1)S(1)}, u32[]{:S(2)}, u32[]{:S(2)}) collective-permute-start(bf16[272,256]{1,0:T(8,128)(2,1)} %get-tuple-element.42), channel_id=1, source_target_pairs={{0,4},{8,12},{16,20},{24,28},{4,0},{12,8},{20,16},{28,24},{1,5},{9... | collective-permute-start | bytes 417800 | tf_op jit(solution)/shard_map/ppermute | solution.py:320
  3.4 3.2 %collective-permute-start = (bf16[272,256]{1,0:T(8,128)(2,1)}, bf16[272,256]{1,0:T(8,128)(2,1)S(1)}, u32[]{:S(2)}, u32[]{:S(2)}) collective-permute-start(bf16[272,256]{1,0:T(8,128)(2,1)} %get-tuple-element.33), channel_id=1, source_target_pairs={{4,8},{12,16},{20,24},{8,4},{16,12},{24,20},{5,9},{13,17},{21,25},... | collective-permute-start | bytes 417800 | tf_op jit(solution)/shard_map/ppermute | solution.py:332
  6.6 1.7 %own.1 = (bf16[512,512]{1,0:T(8,128)(2,1)S(1)}, f32[2,128,512]{2,1,0:T(8,128)S(1)}, bf16[2,128,512]{2,1,0:T(8,128)(2,1)S(1)}) custom-call(s32[8,128]{1,0:T(8,128)S(1)} %copy-done.1, bf16[8,64,448]{2,1,0:T(8,128)(2,1)S(1)} %bitcast.10, bf16[8,64,256]{2,1,0:T(8,128)(2,1)S(1)} %bitcast.14), custom_call_target="tpu_custom_call" | custom-call | flops 1000000000 | bytes 1000000 | tf_op jit(solution)/shard_map/own/pallas_call | solution.py:338
  8.4 0.1 collective-permute-start.1
  8.4 0.5 %scatter.3 = (bf16[2,512,256]{2,1,0:T(8,128)(2,1)S(1)}, bf16[2,512,256]{2,1,0:T(8,128)(2,1)S(1)}) custom-call(s32[8,128]{1,0:T(8,128)S(1)} %copy-done.1, bf16[8,64,448]{2,1,0:T(8,128)(2,1)S(1)} %bitcast.11, bf16[512,512]{1,0:T(8,128)(2,1)S(1)} %get-tuple-element.27.passed.ownt_ref, ...), custom_call_target="tpu_custom_call", output_to_operand_aliasing={{0}: (3, {}), {1}: (4, {})} | custom-call | flops 1000000 | bytes 1000000 | tf_op jit(solution)/shard_map/scatter/pallas_call | solution.py:354
  9.0 0.0 collective-permute-done.5.in_ref
  9.0 1.1 %ghost.3 = (f32[2,128,512]{2,1,0:T(8,128)S(1)}, bf16[2,128,512]{2,1,0:T(8,128)(2,1)S(1)}) custom-call(bf16[2,512,256]{2,1,0:T(8,128)(2,1)S(1)} %get-tuple-element.31.high_ref, bf16[2,512,256]{2,1,0:T(8,128)(2,1)S(1)} %get-tuple-element.32.low_ref, bf16[272,256]{1,0:T(8,128)(2,1)S(1)} %collective-permute-done.5.in_ref, ...), custom_call_target="tpu_custom_call" | custom-call | flops 10000000000 | bytes 1000000 | tf_op jit(solution)/shard_map/ghost/pallas_call | solution.py:368
  10.0 0.5 %collective-permute-start.6 = (bf16[2,128,512]{2,1,0:T(8,128)(2,1)S(1)}, bf16[2,128,512]{2,1,0:T(8,128)(2,1)S(1)}, u32[]{:S(2)}, u32[]{:S(2)}) collective-permute-start(bf16[2,128,512]{2,1,0:T(8,128)(2,1)S(1)} %get-tuple-element.44), channel_id=1, source_target_pairs={{0,1},{1,0},{2,3},{3,2},{4,5},{5,4},{6,7},{7,6},{8,9},{9,8},{10,11... | collective-permute-start | bytes 786440 | tf_op jit(solution)/shard_map/ppermute | solution.py:243
  10.6 0.0 collective-permute-done.1.recv_ref
  10.6 1.6 %collective-permute-start.3 = (bf16[1,128,512]{2,1,0:T(8,128)(2,1)S(1)}, bf16[1,128,512]{2,1,0:T(8,128)(2,1)S(1)}, u32[]{:S(2)}, u32[]{:S(2)}) collective-permute-start(bf16[1,128,512]{2,1,0:T(8,128)(2,1)S(1)} %get-tuple-element.39), channel_id=1, source_target_pairs={{0,2},{1,3},{2,0},{3,1},{4,6},{5,7},{6,4},{7,5},{8,10},{9,11},{10,... | collective-permute-start | bytes 393224 | tf_op jit(solution)/shard_map/ppermute | solution.py:243
  12.2 1.6 %ghost.2 = (f32[2,128,512]{2,1,0:T(8,128)S(1)}, bf16[2,128,512]{2,1,0:T(8,128)(2,1)S(1)}) custom-call(bf16[2,512,256]{2,1,0:T(8,128)(2,1)S(1)} %get-tuple-element.31.high_ref, bf16[2,512,256]{2,1,0:T(8,128)(2,1)S(1)} %get-tuple-element.32.low_ref, bf16[272,256]{1,0:T(8,128)(2,1)S(1)} %collective-permute-done.in_ref, ...), custom_call_target="tpu_custom_call" | custom-call | flops 10000000000 | bytes 1000000 | tf_op jit(solution)/shard_map/ghost/pallas_call | solution.py:368
  13.8 0.1 collective-permute-start.2
  13.9 0.0 collective-permute-done.6.recv_ref
  13.9 0.1 fold.5
  14.0 1.0 %collective-permute-start.7 = (bf16[1,128,512]{2,1,0:T(8,128)(2,1)S(1)}, bf16[1,128,512]{2,1,0:T(8,128)(2,1)S(1)}, u32[]{:S(2)}, u32[]{:S(2)}) collective-permute-start(bf16[1,128,512]{2,1,0:T(8,128)(2,1)S(1)} %get-tuple-element.46), channel_id=1, source_target_pairs={{0,2},{1,3},{2,0},{3,1},{4,6},{5,7},{6,4},{7,5},{8,10},{9,11},{10,... | collective-permute-start | bytes 393224 | tf_op jit(solution)/shard_map/ppermute | solution.py:243
  15.0 1.2 %collective-permute-done.3.recv_ref = bf16[1,128,512]{2,1,0:T(8,128)(2,1)S(1)} collective-permute-done((bf16[1,128,512]{2,1,0:T(8,128)(2,1)S(1)}, bf16[1,128,512]{2,1,0:T(8,128)(2,1)S(1)}, u32[]{:S(2)}, u32[]{:S(2)}) %collective-permute-start.3) | collective-permute-done | bytes 131104 | tf_op jit(solution)/shard_map/ppermute | solution.py:243
  16.1 0.1 fold.4
  16.2 1.6 %collective-permute-start.4 = (bf16[1,128,512]{2,1,0:T(8,128)(2,1)S(1)}, bf16[1,128,512]{2,1,0:T(8,128)(2,1)S(1)}, u32[]{:S(2)}, u32[]{:S(2)}) collective-permute-start(bf16[1,128,512]{2,1,0:T(8,128)(2,1)S(1)} %get-tuple-element.41), channel_id=1, source_target_pairs={{0,2},{1,3},{2,0},{3,1},{4,6},{5,7},{6,4},{7,5},{8,10},{9,11},{10,... | collective-permute-start | bytes 393224 | tf_op jit(solution)/shard_map/ppermute | solution.py:243
  17.8 0.7 %write.3.refs_0_ = f32[128,1536]{1,0:T(8,128)} custom-call(f32[1,128,512]{2,1,0:T(8,128)S(1)} %get-tuple-element.36.refs_2_.keep_ref, bf16[1,128,512]{2,1,0:T(8,128)(2,1)S(1)} %collective-permute-done.3.recv_ref), custom_call_target="tpu_custom_call" | custom-call | flops 100000000 | bytes 1000000 | tf_op jit(solution)/shard_map/write/pallas_call | solution.py:272
  18.6 1.8 %collective-permute-done.7.recv_ref = bf16[1,128,512]{2,1,0:T(8,128)(2,1)S(1)} collective-permute-done((bf16[1,128,512]{2,1,0:T(8,128)(2,1)S(1)}, bf16[1,128,512]{2,1,0:T(8,128)(2,1)S(1)}, u32[]{:S(2)}, u32[]{:S(2)}) %collective-permute-start.7) | collective-permute-done | bytes 131104 | tf_op jit(solution)/shard_map/ppermute | solution.py:243
  20.3 0.7 %write.4.refs_0_ = f32[128,1536]{1,0:T(8,128)} custom-call(f32[1,128,512]{2,1,0:T(8,128)S(1)} %get-tuple-element.45.keep_ref, bf16[1,128,512]{2,1,0:T(8,128)(2,1)S(1)} %collective-permute-done.7.recv_ref, f32[128,1536]{1,0:T(8,128)} %write.3.refs_0_), custom_call_target="tpu_custom_call", output_to_operand_aliasing={{}: (2, {})} | custom-call | flops 100000000 | bytes 1000000 | tf_op jit(solution)/shard_map/write/pallas_call | solution.py:272
  21.1 1.6 %collective-permute-done.4.recv_ref = bf16[1,128,512]{2,1,0:T(8,128)(2,1)S(1)} collective-permute-done((bf16[1,128,512]{2,1,0:T(8,128)(2,1)S(1)}, bf16[1,128,512]{2,1,0:T(8,128)(2,1)S(1)}, u32[]{:S(2)}, u32[]{:S(2)}) %collective-permute-start.4) | collective-permute-done | bytes 131104 | tf_op jit(solution)/shard_map/ppermute | solution.py:243
  22.7 0.7 %write.5 = f32[128,1536]{1,0:T(8,128)} custom-call(f32[1,128,512]{2,1,0:T(8,128)S(1)} %get-tuple-element.40.keep_ref, bf16[1,128,512]{2,1,0:T(8,128)(2,1)S(1)} %collective-permute-done.4.recv_ref, f32[128,1536]{1,0:T(8,128)} %write.4.refs_0_), custom_call_target="tpu_custom_call", output_to_operand_aliasing={{}: (2, {})} | custom-call | flops 100000000 | bytes 1000000 | tf_op jit(solution)/shard_map/write/pallas_call | solution.py:272
  (11 shorter events, 0.1 us)
Async XLA Ops:
  0.0 3.3 %copy-start = (bf16[1,8,64,448]{3,2,1,0:T(8,128)(2,1)S(1)}, bf16[1,8,64,448]{3,2,1,0:T(8,128)(2,1)}, u32[]{:S(2)}) copy-start(bf16[1,8,64,448]{3,2,1,0:T(8,128)(2,1)} %param.6) | copy-start | bytes 1376260
  1.8 1.6 %copy-start.1 = (s32[8,128]{1,0:T(8,128)S(1)}, s32[8,128]{1,0:T(8,128)}, u32[]{:S(2)}) copy-start(s32[8,128]{1,0:T(8,128)} %get-tuple-element.26.info_ref.refs_0_) | copy-start | bytes 12292
  1.8 7.2 %collective-permute-start.5 = (bf16[272,256]{1,0:T(8,128)(2,1)}, bf16[272,256]{1,0:T(8,128)(2,1)S(1)}, u32[]{:S(2)}, u32[]{:S(2)}) collective-permute-start(bf16[272,256]{1,0:T(8,128)(2,1)} %get-tuple-element.42), channel_id=1, source_target_pairs={{0,4},{8,12},{16,20},{24,28},{4,0},{12,8},{20,16},{28,24},{1,5},{9... | collective-permute-start | bytes 417800 | tf_op jit(solution)/shard_map/ppermute | solution.py:320
  3.4 3.3 %copy-start.2 = (bf16[1,8,64,256]{3,2,1,0:T(8,128)(2,1)S(1)}, bf16[1,8,64,256]{3,2,1,0:T(8,128)(2,1)}, u32[]{:S(2)}) copy-start(bf16[1,8,64,256]{3,2,1,0:T(8,128)(2,1)} %param.9) | copy-start | bytes 786436
  3.4 8.9 %collective-permute-start = (bf16[272,256]{1,0:T(8,128)(2,1)}, bf16[272,256]{1,0:T(8,128)(2,1)S(1)}, u32[]{:S(2)}, u32[]{:S(2)}) collective-permute-start(bf16[272,256]{1,0:T(8,128)(2,1)} %get-tuple-element.33), channel_id=1, source_target_pairs={{4,8},{12,16},{20,24},{8,4},{16,12},{24,20},{5,9},{13,17},{21,25},... | collective-permute-start | bytes 417800 | tf_op jit(solution)/shard_map/ppermute | solution.py:332
  8.4 2.2 %collective-permute-start.1 = (bf16[2,128,512]{2,1,0:T(8,128)(2,1)S(1)}, bf16[2,128,512]{2,1,0:T(8,128)(2,1)S(1)}, u32[]{:S(2)}, u32[]{:S(2)}) collective-permute-start(bf16[2,128,512]{2,1,0:T(8,128)(2,1)S(1)} %get-tuple-element.35), channel_id=1, source_target_pairs={{0,1},{1,0},{2,3},{3,2},{4,5},{5,4},{6,7},{7,6},{8,9},{9,8},{10,11... | collective-permute-start | bytes 786440 | tf_op jit(solution)/shard_map/ppermute | solution.py:243
  10.0 3.8 %collective-permute-start.6 = (bf16[2,128,512]{2,1,0:T(8,128)(2,1)S(1)}, bf16[2,128,512]{2,1,0:T(8,128)(2,1)S(1)}, u32[]{:S(2)}, u32[]{:S(2)}) collective-permute-start(bf16[2,128,512]{2,1,0:T(8,128)(2,1)S(1)} %get-tuple-element.44), channel_id=1, source_target_pairs={{0,1},{1,0},{2,3},{3,2},{4,5},{5,4},{6,7},{7,6},{8,9},{9,8},{10,11... | collective-permute-start | bytes 786440 | tf_op jit(solution)/shard_map/ppermute | solution.py:243
  10.6 5.5 %collective-permute-start.3 = (bf16[1,128,512]{2,1,0:T(8,128)(2,1)S(1)}, bf16[1,128,512]{2,1,0:T(8,128)(2,1)S(1)}, u32[]{:S(2)}, u32[]{:S(2)}) collective-permute-start(bf16[1,128,512]{2,1,0:T(8,128)(2,1)S(1)} %get-tuple-element.39), channel_id=1, source_target_pairs={{0,2},{1,3},{2,0},{3,1},{4,6},{5,7},{6,4},{7,5},{8,10},{9,11},{10,... | collective-permute-start | bytes 393224 | tf_op jit(solution)/shard_map/ppermute | solution.py:243
  13.8 2.3 %collective-permute-start.2 = (bf16[2,128,512]{2,1,0:T(8,128)(2,1)S(1)}, bf16[2,128,512]{2,1,0:T(8,128)(2,1)S(1)}, u32[]{:S(2)}, u32[]{:S(2)}) collective-permute-start(bf16[2,128,512]{2,1,0:T(8,128)(2,1)S(1)} %get-tuple-element.38), channel_id=1, source_target_pairs={{0,1},{1,0},{2,3},{3,2},{4,5},{5,4},{6,7},{7,6},{8,9},{9,8},{10,11... | collective-permute-start | bytes 786440 | tf_op jit(solution)/shard_map/ppermute | solution.py:243
  14.0 6.4 %collective-permute-start.7 = (bf16[1,128,512]{2,1,0:T(8,128)(2,1)S(1)}, bf16[1,128,512]{2,1,0:T(8,128)(2,1)S(1)}, u32[]{:S(2)}, u32[]{:S(2)}) collective-permute-start(bf16[1,128,512]{2,1,0:T(8,128)(2,1)S(1)} %get-tuple-element.46), channel_id=1, source_target_pairs={{0,2},{1,3},{2,0},{3,1},{4,6},{5,7},{6,4},{7,5},{8,10},{9,11},{10,... | collective-permute-start | bytes 393224 | tf_op jit(solution)/shard_map/ppermute | solution.py:243
  16.2 6.5 %collective-permute-start.4 = (bf16[1,128,512]{2,1,0:T(8,128)(2,1)S(1)}, bf16[1,128,512]{2,1,0:T(8,128)(2,1)S(1)}, u32[]{:S(2)}, u32[]{:S(2)}) collective-permute-start(bf16[1,128,512]{2,1,0:T(8,128)(2,1)S(1)} %get-tuple-element.41), channel_id=1, source_target_pairs={{0,2},{1,3},{2,0},{3,1},{4,6},{5,7},{6,4},{7,5},{8,10},{9,11},{10,... | collective-permute-start | bytes 393224 | tf_op jit(solution)/shard_map/ppermute | solution.py:243

commit v3 on v2

--- a/solution.py
+++ b/solution.py
@@ -91,14 +91,6 @@
     rows, size = p_ref.shape[0], p_ref.shape[1]
     count = sends.shape[0] // 2
     slots = pcol.shape[0]
-    for n in range(rows):
-        limit = jnp.where(mush[n] > 0, KA, KS)
-        for k in range(KA):
-            info[n, k] = jnp.where(k < limit, acol[k, 0, n], -1)
-        for j in range(slots):
-            info[n, KA + j] = pcol[j, n]
-    passed = pltpu.make_async_copy(info, info_out, sems.at[0])
-    passed.start()
     starts = ((1 - odd) * count, odd * count)
     tail = packed_ref.shape[1] - count * size
     which = lax.broadcasted_iota(jnp.int32, (tail, packed_ref.shape[2]), 0)
@@ -110,13 +102,21 @@
                 cols = jnp.where(which == s * slots + j, pcol[j, row].astype(F32), cols)
         packed_ref[i, count * size :, :] = cols.astype(BF16)
     copies[4].wait()
-    copies = [passed]
+    copies = []
     for i, (out_ref, start) in enumerate(zip((first_ref, second_ref), starts)):
         for s in range(count):
             packed_ref[i, s * size : (s + 1) * size, :] = p_ref[sends[start + s]]
         copies.append(pltpu.make_async_copy(packed_ref.at[i], out_ref, sems.at[1 + i]))
         copies[-1].start()
-    for copy in copies:
+    for n in range(rows):
+        limit = jnp.where(mush[n] > 0, KA, KS)
+        for k in range(KA):
+            info[n, k] = jnp.where(k < limit, acol[k, 0, n], -1)
+        for j in range(slots):
+            info[n, KA + j] = pcol[j, n]
+    passed = pltpu.make_async_copy(info, info_out, sems.at[0])
+    passed.start()
+    for copy in copies + [passed]:
         copy.wait()
 
 
@@ -213,8 +213,8 @@
     finish(ownt_ref, prod_ref[...], keep_ref, send_ref)
 
 
-def fold_kernel(stage, keep_ref, recv_ref, *refs):
-    next_ref, send_ref = refs[-2:]
+def fold_kernel(stage, count, keep_ref, recv_ref, *refs):
+    next_ref, send_ref = refs[count : count + 2]
     bit = (lax.axis_index("gy") >> stage) % 2
     for i in range(next_ref.shape[0]):
         mine, other = 2 * i + bit, 2 * i + 1 - bit
@@ -243,26 +243,32 @@
     return lax.ppermute(value, axis, [(i, i ^ step) for i in range(length) if i ^ step < length])
 
 
-def folded(keep, send, parts, after=()):
+def folded(keep, send, parts, *passed):
     left, share, width = keep.shape
     stage = 0
+    later = ()
     while left > 1:
         recv = swapped(send, "gy", 1 << stage)
         stage += 1
         left //= 2
-        keep, send = pl.pallas_call(
-            functools.partial(fold_kernel, stage),
+        through = passed if stage == 1 else ()
+        count = len(through)
+        keep, send, *through = pl.pallas_call(
+            functools.partial(fold_kernel, stage, count),
             out_shape=(
                 jax.ShapeDtypeStruct((left, share, width), F32),
                 jax.ShapeDtypeStruct((left, share, width), BF16),
-            ),
-            in_specs=[VMEM] * (2 + len(after)),
-            out_specs=(VMEM, VMEM),
+            )
+            + tuple(jax.ShapeDtypeStruct(value.shape, value.dtype) for value in through),
+            in_specs=[VMEM] * (2 + count),
+            out_specs=(VMEM,) * (2 + count),
+            input_output_aliases={2 + i: 2 + i for i in range(count)},
             compiler_params=PARAMS,
             name="fold",
-        )(keep, recv, *after)
-        after = ()
-    return keep, swapped(send, "gy", 1 << stage), keep
+        )(keep, recv, *through)
+        if stage == 1:
+            later, folds = through, keep
+    return keep, swapped(send, "gy", 1 << stage), folds, later
 
 
 def written(order, keep, recv, result):
@@ -350,7 +356,6 @@
         cost_estimate=MEDIUM,
         name="own",
     )(info, ablk, pblk)
-    keep, recv, folds = folded(keep, send, parts)
     high, low = pl.pallas_call(
         functools.partial(scatter_kernel, 0),
         out_shape=(split, split),
@@ -361,25 +366,26 @@
         cost_estimate=TINY,
         name="scatter",
     )(info, ablk, own_t, high, low)
-    pieces = []
-    for order, ghosts in enumerate((first, second)):
-        more = [info, ablk, folds] if order else []
-        pieces.append(
-            pl.pallas_call(
-                functools.partial(ghost_kernel, order),
-                out_shape=partial,
-                in_specs=[VMEM] * (4 + len(more)),
-                out_specs=(VMEM, VMEM),
-                scratch_shapes=[
-                    pltpu.VMEM((count * size, width), BF16),
-                    pltpu.VMEM((rows * size, width), BF16),
-                ]
-                + [pltpu.VMEM((rows * size, count * size), BF16)] * (2 * order),
-                compiler_params=PARAMS,
-                cost_estimate=LONG,
-                name="ghost",
-            )(high, low, ghosts, own_t, *more)
-        )
+
+    def ghost(order, ghosts, *more):
+        return pl.pallas_call(
+            functools.partial(ghost_kernel, order),
+            out_shape=partial,
+            in_specs=[VMEM] * (4 + len(more)),
+            out_specs=(VMEM, VMEM),
+            scratch_shapes=[
+                pltpu.VMEM((count * size, width), BF16),
+                pltpu.VMEM((rows * size, width), BF16),
+            ]
+            + [pltpu.VMEM((rows * size, count * size), BF16)] * (2 * order),
+            compiler_params=PARAMS,
+            cost_estimate=LONG,
+            name="ghost",
+        )(high, low, ghosts, own_t, *more)
+
+    side_keep, side_send = ghost(0, first)
+    keep, recv, folds, (side_send,) = folded(keep, send, parts, side_send)
+    last = ghost(1, second, info, ablk, folds)
     token = pl.pallas_call(
         gate_kernel,
         out_shape=jax.ShapeDtypeStruct((8, LANES), F32),
@@ -389,9 +395,9 @@
         cost_estimate=LONG,
         name="gate",
     )(recv)
-    sides = [folded(*pieces[0], parts), folded(*pieces[1], parts, (token,))]
+    sides = [folded(side_keep, side_send, parts), folded(*last, parts, token)]
     result = written(None, keep, recv, None)
-    for order, (keep, recv, folds) in enumerate(sides):
+    for order, (keep, recv, folds, later) in enumerate(sides):
         result = written(order, keep, recv, result)
     return result[None]
 

time: 23.6 us -> 23.3 us (0.987)
  waiting for transfers between devices: 4.63 us -> 4.35 us
    ppermute x6, waiting for transfers between devices: 4.63 us -> 4.34 us  [swapped(): lax.ppermute(value, axis, [(i, i ^ step) for i in range(length) if i ^ st...]
where the time goes in v3:
time: 23.3 us; the launch traced here: 23.1 us
  starting transfers between devices  9.59 us (41%)
  Pallas kernels  9.07 us (39%)
  waiting for transfers between devices  4.35 us (19%)
    ppermute x6, starting transfers between devices, swapped(): lax.ppermute(value, axis, [(i, i ^ step) for i in range(length) if i ^ st...  4.8 us
    ppermute x6, waiting for transfers between devices, swapped(): lax.ppermute(value, axis, [(i, i ^ step) for i in range(length) if i ^ st...  4.34 us
    ppermute x1, starting transfers between devices, body(): second = lax.ppermute(second, 'gx', uneven + [(j, i) for i, j in uneven])  3.24 us
    pallas_call x2, Pallas kernels, ghost(): pl.pallas_call(functools.partial(ghost_kernel, order), out_shape=partial,...  2.63 us
    pallas_call x3, Pallas kernels, written(): pl.pallas_call(functools.partial(write_kernel, order), out_shape=whole, i...  2.21 us
    pallas_call x1, Pallas kernels, body(): pl.pallas_call(pack_kernel, out_shape=(packed, packed, jax.ShapeDtypeStru...  1.77 us
    pallas_call x1, Pallas kernels, body(): pl.pallas_call(functools.partial(own_kernel, parts), out_shape=(jax.Shape...  1.74 us
    ppermute x1, starting transfers between devices, body(): first = lax.ppermute(first, 'gx', even + [(j, i) for i, j in even])  1.56 us
  transfers between devices with their start and end apart: 8, of which 3 were waited for; matrix products, arithmetic and copies ran while one was open for 0% of the time, Pallas kernels for 28%

profile of v3, /device:TPU:24, one launch (start us, length us, event | category | flops | bytes accessed | tf_op | source)
XLA Modules:
  0.0 23.1 jit_solution(7955572857249512550)
XLA Ops:
  0.0 1.8 %pack.1 = (bf16[272,256]{1,0:T(8,128)(2,1)}, bf16[272,256]{1,0:T(8,128)(2,1)}, s32[8,128]{1,0:T(8,128)}) custom-call(s32[8]{0:T(128)} %bitcast.17, s32[4,8]{1,0:T(4,128)} %bitcast.16, s32[7,1,8]{2,1,0:T(1,128)} %bitcast.15, s32[8]{0:T(128)} %bitcast.18, bf16[8,64,256]{2,1,0:T(8,128)(2,1)} %bitcast.13), custom_call_target="tpu_custom_call" | custom-call | flops 10000000000 | bytes 1000000 | tf_op jit(solution)/shard_map/pack/pallas_call | solution.py:305
  1.8 1.6 %collective-permute-start.2 = (bf16[272,256]{1,0:T(8,128)(2,1)}, bf16[272,256]{1,0:T(8,128)(2,1)S(1)}, u32[]{:S(2)}, u32[]{:S(2)}) collective-permute-start(bf16[272,256]{1,0:T(8,128)(2,1)} %get-tuple-element.37), channel_id=1, source_target_pairs={{0,4},{8,12},{16,20},{24,28},{4,0},{12,8},{20,16},{28,24},{1,5},{9... | collective-permute-start | bytes 417800 | tf_op jit(solution)/shard_map/ppermute | solution.py:326
  3.4 3.2 %collective-permute-start = (bf16[272,256]{1,0:T(8,128)(2,1)}, bf16[272,256]{1,0:T(8,128)(2,1)S(1)}, u32[]{:S(2)}, u32[]{:S(2)}) collective-permute-start(bf16[272,256]{1,0:T(8,128)(2,1)} %get-tuple-element.34), channel_id=1, source_target_pairs={{4,8},{12,16},{20,24},{8,4},{16,12},{24,20},{5,9},{13,17},{21,25},... | collective-permute-start | bytes 417800 | tf_op jit(solution)/shard_map/ppermute | solution.py:338
  6.6 1.7 %own.1 = (bf16[512,512]{1,0:T(8,128)(2,1)S(1)}, f32[2,128,512]{2,1,0:T(8,128)S(1)}, bf16[2,128,512]{2,1,0:T(8,128)(2,1)S(1)}) custom-call(s32[8,128]{1,0:T(8,128)S(1)} %copy-done.1, bf16[8,64,448]{2,1,0:T(8,128)(2,1)S(1)} %bitcast.10, bf16[8,64,256]{2,1,0:T(8,128)(2,1)S(1)} %bitcast.14), custom_call_target="tpu_custom_call" | custom-call | flops 1000000000 | bytes 1000000 | tf_op jit(solution)/shard_map/own/pallas_call | solution.py:344
  8.4 0.1 collective-permute-start.1
  8.4 0.5 %scatter.3 = (bf16[2,512,256]{2,1,0:T(8,128)(2,1)S(1)}, bf16[2,512,256]{2,1,0:T(8,128)(2,1)S(1)}) custom-call(s32[8,128]{1,0:T(8,128)S(1)} %copy-done.1, bf16[8,64,448]{2,1,0:T(8,128)(2,1)S(1)} %bitcast.11, bf16[512,512]{1,0:T(8,128)(2,1)S(1)} %get-tuple-element.28.passed.ownt_ref, ...), custom_call_target="tpu_custom_call", output_to_operand_aliasing={{0}: (3, {}), {1}: (4, {})} | custom-call | flops 1000000 | bytes 1000000 | tf_op jit(solution)/shard_map/scatter/pallas_call | solution.py:359
  9.0 0.0 collective-permute-done.2.in_ref
  9.0 1.1 %ghost.2 = (f32[2,128,512]{2,1,0:T(8,128)S(1)}, bf16[2,128,512]{2,1,0:T(8,128)(2,1)S(1)}) custom-call(bf16[2,512,256]{2,1,0:T(8,128)(2,1)S(1)} %get-tuple-element.32.high_ref, bf16[2,512,256]{2,1,0:T(8,128)(2,1)S(1)} %get-tuple-element.33.low_ref, bf16[272,256]{1,0:T(8,128)(2,1)S(1)} %collective-permute-done.2.in_ref, ...), custom_call_target="tpu_custom_call" | custom-call | flops 10000000000 | bytes 1000000 | tf_op jit(solution)/shard_map/ghost/pallas_call | solution.py:371
  10.1 0.0 collective-permute-done.1.recv_ref
  10.1 0.1 fold.3
  10.1 1.6 %collective-permute-start.4 = (bf16[1,128,512]{2,1,0:T(8,128)(2,1)S(1)}, bf16[1,128,512]{2,1,0:T(8,128)(2,1)S(1)}, u32[]{:S(2)}, u32[]{:S(2)}) collective-permute-start(bf16[1,128,512]{2,1,0:T(8,128)(2,1)S(1)} %get-tuple-element.42), channel_id=1, source_target_pairs={{0,2},{1,3},{2,0},{3,1},{4,6},{5,7},{6,4},{7,5},{8,10},{9,11},{10,... | collective-permute-start | bytes 393224 | tf_op jit(solution)/shard_map/ppermute | solution.py:243
  11.7 0.2 collective-permute-start.6
  11.9 1.6 %ghost.3 = (f32[2,128,512]{2,1,0:T(8,128)S(1)}, bf16[2,128,512]{2,1,0:T(8,128)(2,1)S(1)}) custom-call(bf16[2,512,256]{2,1,0:T(8,128)(2,1)S(1)} %get-tuple-element.32.high_ref, bf16[2,512,256]{2,1,0:T(8,128)(2,1)S(1)} %get-tuple-element.33.low_ref, bf16[272,256]{1,0:T(8,128)(2,1)S(1)} %collective-permute-done.in_ref, ...), custom_call_target="tpu_custom_call" | custom-call | flops 10000000000 | bytes 1000000 | tf_op jit(solution)/shard_map/ghost/pallas_call | solution.py:371
  13.5 0.4 %collective-permute-start.3 = (bf16[2,128,512]{2,1,0:T(8,128)(2,1)S(1)}, bf16[2,128,512]{2,1,0:T(8,128)(2,1)S(1)}, u32[]{:S(2)}, u32[]{:S(2)}) collective-permute-start(bf16[2,128,512]{2,1,0:T(8,128)(2,1)S(1)} %get-tuple-element.41), channel_id=1, source_target_pairs={{0,1},{1,0},{2,3},{3,2},{4,5},{5,4},{6,7},{7,6},{8,9},{9,8},{10,11... | collective-permute-start | bytes 786440 | tf_op jit(solution)/shard_map/ppermute | solution.py:243
  13.9 0.1 fold.5
  13.9 1.0 %collective-permute-start.7 = (bf16[1,128,512]{2,1,0:T(8,128)(2,1)S(1)}, bf16[1,128,512]{2,1,0:T(8,128)(2,1)S(1)}, u32[]{:S(2)}, u32[]{:S(2)}) collective-permute-start(bf16[1,128,512]{2,1,0:T(8,128)(2,1)S(1)} %get-tuple-element.48), channel_id=1, source_target_pairs={{0,2},{1,3},{2,0},{3,1},{4,6},{5,7},{6,4},{7,5},{8,10},{9,11},{10,... | collective-permute-start | bytes 393224 | tf_op jit(solution)/shard_map/ppermute | solution.py:243
  14.9 1.1 %collective-permute-done.4.recv_ref = bf16[1,128,512]{2,1,0:T(8,128)(2,1)S(1)} collective-permute-done((bf16[1,128,512]{2,1,0:T(8,128)(2,1)S(1)}, bf16[1,128,512]{2,1,0:T(8,128)(2,1)S(1)}, u32[]{:S(2)}, u32[]{:S(2)}) %collective-permute-start.4) | collective-permute-done | bytes 131104 | tf_op jit(solution)/shard_map/ppermute | solution.py:243
  16.1 0.1 fold.4
  16.1 1.6 %collective-permute-start.5 = (bf16[1,128,512]{2,1,0:T(8,128)(2,1)S(1)}, bf16[1,128,512]{2,1,0:T(8,128)(2,1)S(1)}, u32[]{:S(2)}, u32[]{:S(2)}) collective-permute-start(bf16[1,128,512]{2,1,0:T(8,128)(2,1)S(1)} %get-tuple-element.44), channel_id=1, source_target_pairs={{0,2},{1,3},{2,0},{3,1},{4,6},{5,7},{6,4},{7,5},{8,10},{9,11},{10,... | collective-permute-start | bytes 393224 | tf_op jit(solution)/shard_map/ppermute | solution.py:243
  17.7 0.7 %write.3.refs_0_ = f32[128,1536]{1,0:T(8,128)} custom-call(f32[1,128,512]{2,1,0:T(8,128)S(1)} %get-tuple-element.39.refs_2_.keep_ref, bf16[1,128,512]{2,1,0:T(8,128)(2,1)S(1)} %collective-permute-done.4.recv_ref), custom_call_target="tpu_custom_call" | custom-call | flops 100000000 | bytes 1000000 | tf_op jit(solution)/shard_map/write/pallas_call | solution.py:278
  18.5 1.9 %collective-permute-done.7.recv_ref = bf16[1,128,512]{2,1,0:T(8,128)(2,1)S(1)} collective-permute-done((bf16[1,128,512]{2,1,0:T(8,128)(2,1)S(1)}, bf16[1,128,512]{2,1,0:T(8,128)(2,1)S(1)}, u32[]{:S(2)}, u32[]{:S(2)}) %collective-permute-start.7) | collective-permute-done | bytes 131104 | tf_op jit(solution)/shard_map/ppermute | solution.py:243
  20.3 0.7 %write.4.refs_0_ = f32[128,1536]{1,0:T(8,128)} custom-call(f32[1,128,512]{2,1,0:T(8,128)S(1)} %get-tuple-element.47.keep_ref, bf16[1,128,512]{2,1,0:T(8,128)(2,1)S(1)} %collective-permute-done.7.recv_ref, f32[128,1536]{1,0:T(8,128)} %write.3.refs_0_), custom_call_target="tpu_custom_call", output_to_operand_aliasing={{}: (2, {})} | custom-call | flops 100000000 | bytes 1000000 | tf_op jit(solution)/shard_map/write/pallas_call | solution.py:278
  21.1 1.3 %collective-permute-done.5.recv_ref = bf16[1,128,512]{2,1,0:T(8,128)(2,1)S(1)} collective-permute-done((bf16[1,128,512]{2,1,0:T(8,128)(2,1)S(1)}, bf16[1,128,512]{2,1,0:T(8,128)(2,1)S(1)}, u32[]{:S(2)}, u32[]{:S(2)}) %collective-permute-start.5) | collective-permute-done | bytes 131104 | tf_op jit(solution)/shard_map/ppermute | solution.py:243
  22.4 0.7 %write.5 = f32[128,1536]{1,0:T(8,128)} custom-call(f32[1,128,512]{2,1,0:T(8,128)S(1)} %get-tuple-element.43.keep_ref, bf16[1,128,512]{2,1,0:T(8,128)(2,1)S(1)} %collective-permute-done.5.recv_ref, f32[128,1536]{1,0:T(8,128)} %write.4.refs_0_), custom_call_target="tpu_custom_call", output_to_operand_aliasing={{}: (2, {})} | custom-call | flops 100000000 | bytes 1000000 | tf_op jit(solution)/shard_map/write/pallas_call | solution.py:278
  (11 shorter events, 0.0 us)
Async XLA Ops:
  0.0 3.3 %copy-start = (bf16[1,8,64,448]{3,2,1,0:T(8,128)(2,1)S(1)}, bf16[1,8,64,448]{3,2,1,0:T(8,128)(2,1)}, u32[]{:S(2)}) copy-start(bf16[1,8,64,448]{3,2,1,0:T(8,128)(2,1)} %param.6) | copy-start | bytes 1376260
  1.8 1.6 %copy-start.1 = (s32[8,128]{1,0:T(8,128)S(1)}, s32[8,128]{1,0:T(8,128)}, u32[]{:S(2)}) copy-start(s32[8,128]{1,0:T(8,128)} %get-tuple-element.27.info_ref.refs_0_) | copy-start | bytes 12292
  1.8 7.2 %collective-permute-start.2 = (bf16[272,256]{1,0:T(8,128)(2,1)}, bf16[272,256]{1,0:T(8,128)(2,1)S(1)}, u32[]{:S(2)}, u32[]{:S(2)}) collective-permute-start(bf16[272,256]{1,0:T(8,128)(2,1)} %get-tuple-element.37), channel_id=1, source_target_pairs={{0,4},{8,12},{16,20},{24,28},{4,0},{12,8},{20,16},{28,24},{1,5},{9... | collective-permute-start | bytes 417800 | tf_op jit(solution)/shard_map/ppermute | solution.py:326
  3.4 3.3 %copy-start.2 = (bf16[1,8,64,256]{3,2,1,0:T(8,128)(2,1)S(1)}, bf16[1,8,64,256]{3,2,1,0:T(8,128)(2,1)}, u32[]{:S(2)}) copy-start(bf16[1,8,64,256]{3,2,1,0:T(8,128)(2,1)} %param.9) | copy-start | bytes 786436
  3.4 8.5 %collective-permute-start = (bf16[272,256]{1,0:T(8,128)(2,1)}, bf16[272,256]{1,0:T(8,128)(2,1)S(1)}, u32[]{:S(2)}, u32[]{:S(2)}) collective-permute-start(bf16[272,256]{1,0:T(8,128)(2,1)} %get-tuple-element.34), channel_id=1, source_target_pairs={{4,8},{12,16},{20,24},{8,4},{16,12},{24,20},{5,9},{13,17},{21,25},... | collective-permute-start | bytes 417800 | tf_op jit(solution)/shard_map/ppermute | solution.py:338
  8.4 1.7 %collective-permute-start.1 = (bf16[2,128,512]{2,1,0:T(8,128)(2,1)S(1)}, bf16[2,128,512]{2,1,0:T(8,128)(2,1)S(1)}, u32[]{:S(2)}, u32[]{:S(2)}) collective-permute-start(bf16[2,128,512]{2,1,0:T(8,128)(2,1)S(1)} %get-tuple-element.36), channel_id=1, source_target_pairs={{0,1},{1,0},{2,3},{3,2},{4,5},{5,4},{6,7},{7,6},{8,9},{9,8},{10,11... | collective-permute-start | bytes 786440 | tf_op jit(solution)/shard_map/ppermute | solution.py:243
  10.1 5.9 %collective-permute-start.4 = (bf16[1,128,512]{2,1,0:T(8,128)(2,1)S(1)}, bf16[1,128,512]{2,1,0:T(8,128)(2,1)S(1)}, u32[]{:S(2)}, u32[]{:S(2)}) collective-permute-start(bf16[1,128,512]{2,1,0:T(8,128)(2,1)S(1)} %get-tuple-element.42), channel_id=1, source_target_pairs={{0,2},{1,3},{2,0},{3,1},{4,6},{5,7},{6,4},{7,5},{8,10},{9,11},{10,... | collective-permute-start | bytes 393224 | tf_op jit(solution)/shard_map/ppermute | solution.py:243
  11.7 2.2 %collective-permute-start.6 = (bf16[2,128,512]{2,1,0:T(8,128)(2,1)S(1)}, bf16[2,128,512]{2,1,0:T(8,128)(2,1)S(1)}, u32[]{:S(2)}, u32[]{:S(2)}) collective-permute-start(bf16[2,128,512]{2,1,0:T(8,128)(2,1)S(1)} %get-tuple-element.46), channel_id=1, source_target_pairs={{0,1},{1,0},{2,3},{3,2},{4,5},{5,4},{6,7},{7,6},{8,9},{9,8},{10,11... | collective-permute-start | bytes 786440 | tf_op jit(solution)/shard_map/ppermute | solution.py:243
  13.5 2.6 %collective-permute-start.3 = (bf16[2,128,512]{2,1,0:T(8,128)(2,1)S(1)}, bf16[2,128,512]{2,1,0:T(8,128)(2,1)S(1)}, u32[]{:S(2)}, u32[]{:S(2)}) collective-permute-start(bf16[2,128,512]{2,1,0:T(8,128)(2,1)S(1)} %get-tuple-element.41), channel_id=1, source_target_pairs={{0,1},{1,0},{2,3},{3,2},{4,5},{5,4},{6,7},{7,6},{8,9},{9,8},{10,11... | collective-permute-start | bytes 786440 | tf_op jit(solution)/shard_map/ppermute | solution.py:243
  13.9 6.4 %collective-permute-start.7 = (bf16[1,128,512]{2,1,0:T(8,128)(2,1)S(1)}, bf16[1,128,512]{2,1,0:T(8,128)(2,1)S(1)}, u32[]{:S(2)}, u32[]{:S(2)}) collective-permute-start(bf16[1,128,512]{2,1,0:T(8,128)(2,1)S(1)} %get-tuple-element.48), channel_id=1, source_target_pairs={{0,2},{1,3},{2,0},{3,1},{4,6},{5,7},{6,4},{7,5},{8,10},{9,11},{10,... | collective-permute-start | bytes 393224 | tf_op jit(solution)/shard_map/ppermute | solution.py:243
  16.1 6.3 %collective-permute-start.5 = (bf16[1,128,512]{2,1,0:T(8,128)(2,1)S(1)}, bf16[1,128,512]{2,1,0:T(8,128)(2,1)S(1)}, u32[]{:S(2)}, u32[]{:S(2)}) collective-permute-start(bf16[1,128,512]{2,1,0:T(8,128)(2,1)S(1)} %get-tuple-element.44), channel_id=1, source_target_pairs={{0,2},{1,3},{2,0},{3,1},{4,6},{5,7},{6,4},{7,5},{8,10},{9,11},{10,... | collective-permute-start | bytes 393224 | tf_op jit(solution)/shard_map/ppermute | solution.py:243

commit v4 on v3

--- a/solution.py
+++ b/solution.py
@@ -162,13 +162,18 @@
             low_ref[at, spot] = (tile - high.astype(F32)).astype(BF16)
 
 
-def scatter_kernel(when, info_ref, a_ref, passed, *refs):
-    high_ref, low_ref = refs[-3:-1] if when else refs[-2:]
-
-    @pl.when(lax.axis_index("gx") % 2 == when)
-    def _():
-        for order in range(1 + when):
-            scatter(order, info_ref, a_ref, high_ref.at[order], low_ref.at[order])
+def scatter_kernel(late, info_ref, a_ref, passed, *refs):
+    high_ref, low_ref = refs[-2:] if late else refs[-3:-1]
+    place = lax.axis_index("gx")
+
+    def side(order):
+        scatter(order, info_ref, a_ref, high_ref.at[order], low_ref.at[order])
+
+    if late:
+        pl.when(place % 2 == 0)(lambda: side(0))
+        pl.when((place % 2 == 1) | (place == 0))(lambda: side(1))
+    else:
+        pl.when(place % 2 == 1)(lambda: side(0))
 
 
 def ghost_kernel(order, high_ref, low_ref, in_ref, ownt_ref, *refs):
@@ -197,14 +202,15 @@
             prod_ref[at, :] = value.astype(BF16)
 
     if order:
-        odd = lax.axis_index("gx") % 2
-
-        @pl.when(odd == 0)
+        place = lax.axis_index("gx")
+        open_side = (place % 2 == 0) & (place > 0)
+
+        @pl.when(open_side)
         def _():
             scatter(1, info_ref, a_ref, mine_high, mine_low)
             product(mine_high, mine_low)
 
-        @pl.when(odd == 1)
+        @pl.when(jnp.logical_not(open_side))
         def _():
             product(high_ref.at[1], low_ref.at[1])
 
@@ -223,15 +229,20 @@
 
 
 def write_kernel(order, keep_ref, recv_ref, *refs):
-    out_ref, sum_ref, sem = refs[-3:]
+    out_ref, sum_ref, sems = refs[-3:]
     odd = lax.axis_index("gx") % 2
     third = 1 if order is None else 2 * odd if order else 2 - 2 * odd
-    width = sum_ref.shape[1]
-    sum_ref[...] = keep_ref[0] + recv_ref[0].astype(F32)
+    share, width = sum_ref.shape
     spot = pl.ds(pl.multiple_of(third * width, width), width)
-    copy = pltpu.make_async_copy(sum_ref, out_ref.at[:, spot], sem)
-    copy.start()
-    copy.wait()
+    count = sems.shape[0]
+    copies = []
+    for i in range(count):
+        at = slice(i * share // count, (i + 1) * share // count)
+        sum_ref[at, :] = keep_ref[0, at, :] + recv_ref[0, at, :].astype(F32)
+        copies.append(pltpu.make_async_copy(sum_ref.at[at], out_ref.at[at, spot], sems.at[i]))
+        copies[-1].start()
+    for copy in copies:
+        copy.wait()
 
 
 def gate_kernel(recv_ref, token_ref):
@@ -281,7 +292,10 @@
         in_specs=[VMEM, VMEM] if start else [VMEM, VMEM, HBM],
         out_specs=HBM,
         input_output_aliases={} if start else {2: 0},
-        scratch_shapes=[pltpu.VMEM((share, width), F32), pltpu.SemaphoreType.DMA],
+        scratch_shapes=[
+            pltpu.VMEM((share, width), F32),
+            pltpu.SemaphoreType.DMA((max(1, min(4, share // 16)),)),
+        ],
         compiler_params=PARAMS,
         cost_estimate=SHORT,
         name="write",
@@ -326,7 +340,7 @@
     first = lax.ppermute(first, "gx", even + [(j, i) for i, j in even])
     split = jax.ShapeDtypeStruct((2, rows * size, count * size), BF16)
     high, low, second = pl.pallas_call(
-        functools.partial(scatter_kernel, 1),
+        functools.partial(scatter_kernel, False),
         out_shape=(split, split, packed),
         in_specs=[VMEM, VMEM, HBM],
         out_specs=(VMEM, VMEM, HBM),
@@ -357,7 +371,7 @@
         name="own",
     )(info, ablk, pblk)
     high, low = pl.pallas_call(
-        functools.partial(scatter_kernel, 0),
+        functools.partial(scatter_kernel, True),
         out_shape=(split, split),
         in_specs=[VMEM, VMEM, VMEM, VMEM, VMEM],
         out_specs=(VMEM, VMEM),

time: 23.3 us -> 23.3 us (level); the launches traced: 23.1 us -> 22.9 us
  waiting for transfers between devices: 4.35 us -> 4.06 us
    ppermute x1, starting transfers between devices: 3.24 us -> 2.91 us  [body(): second = lax.ppermute(second, 'gx', uneven + [(j, i) for i, j in uneven])]
    ppermute x6, starting transfers between devices: 4.8 us -> 5.12 us  [swapped(): lax.ppermute(value, axis, [(i, i ^ step) for i in range(length) if i ^ st...]
    ppermute x6, waiting for transfers between devices: 4.34 us -> 4.02 us  [swapped(): lax.ppermute(value, axis, [(i, i ^ step) for i in range(length) if i ^ st...]
  transfers between devices with their start and end apart: 8 -> 8, of which waited for: 3 -> 3; matrix products, arithmetic and copies ran while one was open for 0% -> 0% of each run, Pallas kernels for 28% -> 29%
where the time goes in v4:
time: 23.3 us; the launch traced here: 22.9 us
  starting transfers between devices  9.59 us (41%)
  Pallas kernels  9.08 us (39%)
  waiting for transfers between devices  4.06 us (17%)
    ppermute x6, starting transfers between devices, swapped(): lax.ppermute(value, axis, [(i, i ^ step) for i in range(length) if i ^ st...  5.12 us
    ppermute x6, waiting for transfers between devices, swapped(): lax.ppermute(value, axis, [(i, i ^ step) for i in range(length) if i ^ st...  4.02 us
    ppermute x1, starting transfers between devices, body(): second = lax.ppermute(second, 'gx', uneven + [(j, i) for i, j in uneven])  2.91 us
    pallas_call x2, Pallas kernels, ghost(): pl.pallas_call(functools.partial(ghost_kernel, order), out_shape=partial,...  2.62 us
    pallas_call x3, Pallas kernels, written(): pl.pallas_call(functools.partial(write_kernel, order), out_shape=whole, i...  2.24 us
    pallas_call x1, Pallas kernels, body(): pl.pallas_call(pack_kernel, out_shape=(packed, packed, jax.ShapeDtypeStru...  1.77 us
    pallas_call x1, Pallas kernels, body(): pl.pallas_call(functools.partial(own_kernel, parts), out_shape=(jax.Shape...  1.73 us
    ppermute x1, starting transfers between devices, body(): first = lax.ppermute(first, 'gx', even + [(j, i) for i, j in even])  1.56 us
  transfers between devices with their start and end apart: 8, of which 3 were waited for; matrix products, arithmetic and copies ran while one was open for 0% of the time, Pallas kernels for 29%

profile of v4, /device:TPU:24, one launch (start us, length us, event | category | flops | bytes accessed | tf_op | source)
XLA Modules:
  0.0 22.9 jit_solution(167911654950210404)
XLA Ops:
  0.0 1.8 %pack.1 = (bf16[272,256]{1,0:T(8,128)(2,1)}, bf16[272,256]{1,0:T(8,128)(2,1)}, s32[8,128]{1,0:T(8,128)}) custom-call(s32[8]{0:T(128)} %bitcast.17, s32[4,8]{1,0:T(4,128)} %bitcast.16, s32[7,1,8]{2,1,0:T(1,128)} %bitcast.15, s32[8]{0:T(128)} %bitcast.18, bf16[8,64,256]{2,1,0:T(8,128)(2,1)} %bitcast.13), custom_call_target="tpu_custom_call" | custom-call | flops 10000000000 | bytes 1000000 | tf_op jit(solution)/shard_map/pack/pallas_call | solution.py:319
  1.8 1.6 %collective-permute-start.2 = (bf16[272,256]{1,0:T(8,128)(2,1)}, bf16[272,256]{1,0:T(8,128)(2,1)S(1)}, u32[]{:S(2)}, u32[]{:S(2)}) collective-permute-start(bf16[272,256]{1,0:T(8,128)(2,1)} %get-tuple-element.37), channel_id=1, source_target_pairs={{0,4},{8,12},{16,20},{24,28},{4,0},{12,8},{20,16},{28,24},{1,5},{9... | collective-permute-start | bytes 417800 | tf_op jit(solution)/shard_map/ppermute | solution.py:340
  3.4 2.9 %collective-permute-start = (bf16[272,256]{1,0:T(8,128)(2,1)}, bf16[272,256]{1,0:T(8,128)(2,1)S(1)}, u32[]{:S(2)}, u32[]{:S(2)}) collective-permute-start(bf16[272,256]{1,0:T(8,128)(2,1)} %get-tuple-element.34), channel_id=1, source_target_pairs={{4,8},{12,16},{20,24},{8,4},{16,12},{24,20},{5,9},{13,17},{21,25},... | collective-permute-start | bytes 417800 | tf_op jit(solution)/shard_map/ppermute | solution.py:352
  6.3 1.7 %own.1 = (bf16[512,512]{1,0:T(8,128)(2,1)S(1)}, f32[2,128,512]{2,1,0:T(8,128)S(1)}, bf16[2,128,512]{2,1,0:T(8,128)(2,1)S(1)}) custom-call(s32[8,128]{1,0:T(8,128)S(1)} %copy-done.1, bf16[8,64,448]{2,1,0:T(8,128)(2,1)S(1)} %bitcast.10, bf16[8,64,256]{2,1,0:T(8,128)(2,1)S(1)} %bitcast.14), custom_call_target="tpu_custom_call" | custom-call | flops 1000000000 | bytes 1000000 | tf_op jit(solution)/shard_map/own/pallas_call | solution.py:358
  8.0 0.1 collective-permute-start.1
  8.1 0.5 %scatter.3 = (bf16[2,512,256]{2,1,0:T(8,128)(2,1)S(1)}, bf16[2,512,256]{2,1,0:T(8,128)(2,1)S(1)}) custom-call(s32[8,128]{1,0:T(8,128)S(1)} %copy-done.1, bf16[8,64,448]{2,1,0:T(8,128)(2,1)S(1)} %bitcast.11, bf16[512,512]{1,0:T(8,128)(2,1)S(1)} %get-tuple-element.28.passed.ownt_ref, ...), custom_call_target="tpu_custom_call", output_to_operand_aliasing={{0}: (3, {}), {1}: (4, {})} | custom-call | flops 1000000 | bytes 1000000 | tf_op jit(solution)/shard_map/scatter/pallas_call | solution.py:373
  8.7 0.0 collective-permute-done.2.in_ref
  8.7 1.0 %ghost.2 = (f32[2,128,512]{2,1,0:T(8,128)S(1)}, bf16[2,128,512]{2,1,0:T(8,128)(2,1)S(1)}) custom-call(bf16[2,512,256]{2,1,0:T(8,128)(2,1)S(1)} %get-tuple-element.32.high_ref, bf16[2,512,256]{2,1,0:T(8,128)(2,1)S(1)} %get-tuple-element.33.low_ref, bf16[272,256]{1,0:T(8,128)(2,1)S(1)} %collective-permute-done.2.in_ref, ...), custom_call_target="tpu_custom_call" | custom-call | flops 10000000000 | bytes 1000000 | tf_op jit(solution)/shard_map/ghost/pallas_call | solution.py:385
  9.7 0.1 fold.3
  9.8 1.6 %collective-permute-start.4 = (bf16[1,128,512]{2,1,0:T(8,128)(2,1)S(1)}, bf16[1,128,512]{2,1,0:T(8,128)(2,1)S(1)}, u32[]{:S(2)}, u32[]{:S(2)}) collective-permute-start(bf16[1,128,512]{2,1,0:T(8,128)(2,1)S(1)} %get-tuple-element.42), channel_id=1, source_target_pairs={{0,2},{1,3},{2,0},{3,1},{4,6},{5,7},{6,4},{7,5},{8,10},{9,11},{10,... | collective-permute-start | bytes 393224 | tf_op jit(solution)/shard_map/ppermute | solution.py:254
  11.4 0.2 collective-permute-start.6
  11.6 0.0 collective-permute-done.in_ref
  11.6 1.6 %ghost.3 = (f32[2,128,512]{2,1,0:T(8,128)S(1)}, bf16[2,128,512]{2,1,0:T(8,128)(2,1)S(1)}) custom-call(bf16[2,512,256]{2,1,0:T(8,128)(2,1)S(1)} %get-tuple-element.32.high_ref, bf16[2,512,256]{2,1,0:T(8,128)(2,1)S(1)} %get-tuple-element.33.low_ref, bf16[272,256]{1,0:T(8,128)(2,1)S(1)} %collective-permute-done.in_ref, ...), custom_call_target="tpu_custom_call" | custom-call | flops 10000000000 | bytes 1000000 | tf_op jit(solution)/shard_map/ghost/pallas_call | solution.py:385
  13.2 0.3 %collective-permute-start.3 = (bf16[2,128,512]{2,1,0:T(8,128)(2,1)S(1)}, bf16[2,128,512]{2,1,0:T(8,128)(2,1)S(1)}, u32[]{:S(2)}, u32[]{:S(2)}) collective-permute-start(bf16[2,128,512]{2,1,0:T(8,128)(2,1)S(1)} %get-tuple-element.41), channel_id=1, source_target_pairs={{0,1},{1,0},{2,3},{3,2},{4,5},{5,4},{6,7},{7,6},{8,9},{9,8},{10,11... | collective-permute-start | bytes 786440 | tf_op jit(solution)/shard_map/ppermute | solution.py:254
  13.6 0.1 fold.5
  13.6 1.3 %collective-permute-start.7 = (bf16[1,128,512]{2,1,0:T(8,128)(2,1)S(1)}, bf16[1,128,512]{2,1,0:T(8,128)(2,1)S(1)}, u32[]{:S(2)}, u32[]{:S(2)}) collective-permute-start(bf16[1,128,512]{2,1,0:T(8,128)(2,1)S(1)} %get-tuple-element.48), channel_id=1, source_target_pairs={{0,2},{1,3},{2,0},{3,1},{4,6},{5,7},{6,4},{7,5},{8,10},{9,11},{10,... | collective-permute-start | bytes 393224 | tf_op jit(solution)/shard_map/ppermute | solution.py:254
  14.9 0.8 %collective-permute-done.4.recv_ref = bf16[1,128,512]{2,1,0:T(8,128)(2,1)S(1)} collective-permute-done((bf16[1,128,512]{2,1,0:T(8,128)(2,1)S(1)}, bf16[1,128,512]{2,1,0:T(8,128)(2,1)S(1)}, u32[]{:S(2)}, u32[]{:S(2)}) %collective-permute-start.4) | collective-permute-done | bytes 131104 | tf_op jit(solution)/shard_map/ppermute | solution.py:254
  15.8 0.1 fold.4
  15.8 1.6 %collective-permute-start.5 = (bf16[1,128,512]{2,1,0:T(8,128)(2,1)S(1)}, bf16[1,128,512]{2,1,0:T(8,128)(2,1)S(1)}, u32[]{:S(2)}, u32[]{:S(2)}) collective-permute-start(bf16[1,128,512]{2,1,0:T(8,128)(2,1)S(1)} %get-tuple-element.44), channel_id=1, source_target_pairs={{0,2},{1,3},{2,0},{3,1},{4,6},{5,7},{6,4},{7,5},{8,10},{9,11},{10,... | collective-permute-start | bytes 393224 | tf_op jit(solution)/shard_map/ppermute | solution.py:254
  17.4 0.7 %write.3.refs_0_ = f32[128,1536]{1,0:T(8,128)} custom-call(f32[1,128,512]{2,1,0:T(8,128)S(1)} %get-tuple-element.39.refs_2_.keep_ref, bf16[1,128,512]{2,1,0:T(8,128)(2,1)S(1)} %collective-permute-done.4.recv_ref), custom_call_target="tpu_custom_call" | custom-call | flops 100000000 | bytes 1000000 | tf_op jit(solution)/shard_map/write/pallas_call | solution.py:289
  18.1 1.9 %collective-permute-done.7.recv_ref = bf16[1,128,512]{2,1,0:T(8,128)(2,1)S(1)} collective-permute-done((bf16[1,128,512]{2,1,0:T(8,128)(2,1)S(1)}, bf16[1,128,512]{2,1,0:T(8,128)(2,1)S(1)}, u32[]{:S(2)}, u32[]{:S(2)}) %collective-permute-start.7) | collective-permute-done | bytes 131104 | tf_op jit(solution)/shard_map/ppermute | solution.py:254
  20.0 0.8 %write.4.refs_0_ = f32[128,1536]{1,0:T(8,128)} custom-call(f32[1,128,512]{2,1,0:T(8,128)S(1)} %get-tuple-element.47.keep_ref, bf16[1,128,512]{2,1,0:T(8,128)(2,1)S(1)} %collective-permute-done.7.recv_ref, f32[128,1536]{1,0:T(8,128)} %write.3.refs_0_), custom_call_target="tpu_custom_call", output_to_operand_aliasing={{}: (2, {})} | custom-call | flops 100000000 | bytes 1000000 | tf_op jit(solution)/shard_map/write/pallas_call | solution.py:289
  20.8 1.4 %collective-permute-done.5.recv_ref = bf16[1,128,512]{2,1,0:T(8,128)(2,1)S(1)} collective-permute-done((bf16[1,128,512]{2,1,0:T(8,128)(2,1)S(1)}, bf16[1,128,512]{2,1,0:T(8,128)(2,1)S(1)}, u32[]{:S(2)}, u32[]{:S(2)}) %collective-permute-start.5) | collective-permute-done | bytes 131104 | tf_op jit(solution)/shard_map/ppermute | solution.py:254
  22.1 0.8 %write.5 = f32[128,1536]{1,0:T(8,128)} custom-call(f32[1,128,512]{2,1,0:T(8,128)S(1)} %get-tuple-element.43.keep_ref, bf16[1,128,512]{2,1,0:T(8,128)(2,1)S(1)} %collective-permute-done.5.recv_ref, f32[128,1536]{1,0:T(8,128)} %write.4.refs_0_), custom_call_target="tpu_custom_call", output_to_operand_aliasing={{}: (2, {})} | custom-call | flops 100000000 | bytes 1000000 | tf_op jit(solution)/shard_map/write/pallas_call | solution.py:289
  (11 shorter events, 0.0 us)
Async XLA Ops:
  0.0 3.3 %copy-start = (bf16[1,8,64,448]{3,2,1,0:T(8,128)(2,1)S(1)}, bf16[1,8,64,448]{3,2,1,0:T(8,128)(2,1)}, u32[]{:S(2)}) copy-start(bf16[1,8,64,448]{3,2,1,0:T(8,128)(2,1)} %param.6) | copy-start | bytes 1376260
  1.8 1.6 %copy-start.1 = (s32[8,128]{1,0:T(8,128)S(1)}, s32[8,128]{1,0:T(8,128)}, u32[]{:S(2)}) copy-start(s32[8,128]{1,0:T(8,128)} %get-tuple-element.27.info_ref.refs_0_) | copy-start | bytes 12292
  1.8 6.9 %collective-permute-start.2 = (bf16[272,256]{1,0:T(8,128)(2,1)}, bf16[272,256]{1,0:T(8,128)(2,1)S(1)}, u32[]{:S(2)}, u32[]{:S(2)}) collective-permute-start(bf16[272,256]{1,0:T(8,128)(2,1)} %get-tuple-element.37), channel_id=1, source_target_pairs={{0,4},{8,12},{16,20},{24,28},{4,0},{12,8},{20,16},{28,24},{1,5},{9... | collective-permute-start | bytes 417800 | tf_op jit(solution)/shard_map/ppermute | solution.py:340
  3.4 2.9 %copy-start.2 = (bf16[1,8,64,256]{3,2,1,0:T(8,128)(2,1)S(1)}, bf16[1,8,64,256]{3,2,1,0:T(8,128)(2,1)}, u32[]{:S(2)}) copy-start(bf16[1,8,64,256]{3,2,1,0:T(8,128)(2,1)} %param.9) | copy-start | bytes 786436
  3.4 8.3 %collective-permute-start = (bf16[272,256]{1,0:T(8,128)(2,1)}, bf16[272,256]{1,0:T(8,128)(2,1)S(1)}, u32[]{:S(2)}, u32[]{:S(2)}) collective-permute-start(bf16[272,256]{1,0:T(8,128)(2,1)} %get-tuple-element.34), channel_id=1, source_target_pairs={{4,8},{12,16},{20,24},{8,4},{16,12},{24,20},{5,9},{13,17},{21,25},... | collective-permute-start | bytes 417800 | tf_op jit(solution)/shard_map/ppermute | solution.py:352
  8.0 1.7 %collective-permute-start.1 = (bf16[2,128,512]{2,1,0:T(8,128)(2,1)S(1)}, bf16[2,128,512]{2,1,0:T(8,128)(2,1)S(1)}, u32[]{:S(2)}, u32[]{:S(2)}) collective-permute-start(bf16[2,128,512]{2,1,0:T(8,128)(2,1)S(1)} %get-tuple-element.36), channel_id=1, source_target_pairs={{0,1},{1,0},{2,3},{3,2},{4,5},{5,4},{6,7},{7,6},{8,9},{9,8},{10,11... | collective-permute-start | bytes 786440 | tf_op jit(solution)/shard_map/ppermute | solution.py:254
  9.8 5.9 %collective-permute-start.4 = (bf16[1,128,512]{2,1,0:T(8,128)(2,1)S(1)}, bf16[1,128,512]{2,1,0:T(8,128)(2,1)S(1)}, u32[]{:S(2)}, u32[]{:S(2)}) collective-permute-start(bf16[1,128,512]{2,1,0:T(8,128)(2,1)S(1)} %get-tuple-element.42), channel_id=1, source_target_pairs={{0,2},{1,3},{2,0},{3,1},{4,6},{5,7},{6,4},{7,5},{8,10},{9,11},{10,... | collective-permute-start | bytes 393224 | tf_op jit(solution)/shard_map/ppermute | solution.py:254
  11.4 2.2 %collective-permute-start.6 = (bf16[2,128,512]{2,1,0:T(8,128)(2,1)S(1)}, bf16[2,128,512]{2,1,0:T(8,128)(2,1)S(1)}, u32[]{:S(2)}, u32[]{:S(2)}) collective-permute-start(bf16[2,128,512]{2,1,0:T(8,128)(2,1)S(1)} %get-tuple-element.46), channel_id=1, source_target_pairs={{0,1},{1,0},{2,3},{3,2},{4,5},{5,4},{6,7},{7,6},{8,9},{9,8},{10,11... | collective-permute-start | bytes 786440 | tf_op jit(solution)/shard_map/ppermute | solution.py:254
  13.2 2.6 %collective-permute-start.3 = (bf16[2,128,512]{2,1,0:T(8,128)(2,1)S(1)}, bf16[2,128,512]{2,1,0:T(8,128)(2,1)S(1)}, u32[]{:S(2)}, u32[]{:S(2)}) collective-permute-start(bf16[2,128,512]{2,1,0:T(8,128)(2,1)S(1)} %get-tuple-element.41), channel_id=1, source_target_pairs={{0,1},{1,0},{2,3},{3,2},{4,5},{5,4},{6,7},{7,6},{8,9},{9,8},{10,11... | collective-permute-start | bytes 786440 | tf_op jit(solution)/shard_map/ppermute | solution.py:254
  13.6 6.4 %collective-permute-start.7 = (bf16[1,128,512]{2,1,0:T(8,128)(2,1)S(1)}, bf16[1,128,512]{2,1,0:T(8,128)(2,1)S(1)}, u32[]{:S(2)}, u32[]{:S(2)}) collective-permute-start(bf16[1,128,512]{2,1,0:T(8,128)(2,1)S(1)} %get-tuple-element.48), channel_id=1, source_target_pairs={{0,2},{1,3},{2,0},{3,1},{4,6},{5,7},{6,4},{7,5},{8,10},{9,11},{10,... | collective-permute-start | bytes 393224 | tf_op jit(solution)/shard_map/ppermute | solution.py:254
  15.8 6.3 %collective-permute-start.5 = (bf16[1,128,512]{2,1,0:T(8,128)(2,1)S(1)}, bf16[1,128,512]{2,1,0:T(8,128)(2,1)S(1)}, u32[]{:S(2)}, u32[]{:S(2)}) collective-permute-start(bf16[1,128,512]{2,1,0:T(8,128)(2,1)S(1)} %get-tuple-element.44), channel_id=1, source_target_pairs={{0,2},{1,3},{2,0},{3,1},{4,6},{5,7},{6,4},{7,5},{8,10},{9,11},{10,... | collective-permute-start | bytes 393224 | tf_op jit(solution)/shard_map/ppermute | solution.py:254

commit v5 on v4

--- a/solution.py
+++ b/solution.py
@@ -163,11 +163,11 @@
 
 
 def scatter_kernel(late, info_ref, a_ref, passed, *refs):
-    high_ref, low_ref = refs[-2:] if late else refs[-3:-1]
+    laid = refs[-4:] if late else refs[-5:-1]
     place = lax.axis_index("gx")
 
     def side(order):
-        scatter(order, info_ref, a_ref, high_ref.at[order], low_ref.at[order])
+        scatter(order, info_ref, a_ref, *laid[2 * order : 2 * order + 2])
 
     if late:
         pl.when(place % 2 == 0)(lambda: side(0))
@@ -176,11 +176,12 @@
         pl.when(place % 2 == 1)(lambda: side(0))
 
 
-def ghost_kernel(order, high_ref, low_ref, in_ref, ownt_ref, *refs):
-    if order:
-        info_ref, a_ref, after, keep_ref, send_ref, ext_ref, prod_ref, mine_high, mine_low = refs
-    else:
-        keep_ref, send_ref, ext_ref, prod_ref = refs
+def second_kernel(info_ref, a_ref, after, *refs):
+    place = lax.axis_index("gx")
+    pl.when((place % 2 == 0) & (place > 0))(lambda: scatter(1, info_ref, a_ref, *refs[-2:]))
+
+
+def ghost_kernel(high_ref, low_ref, in_ref, ownt_ref, keep_ref, send_ref, ext_ref, prod_ref):
     width = ownt_ref.shape[0]
     size = width // NCOL
     slots = in_ref.shape[1] // size
@@ -192,30 +193,13 @@
         for c, tile in enumerate(spread(in_ref[at, :], masks, width)):
             ext_ref[at, c * WIDE : (c + 1) * WIDE] = tile.astype(BF16)
 
-    def product(high, low):
-        ext = ext_ref[...]
-        step = prod_ref.shape[0] // 2
-        for m in range(2):
-            at = slice(m * step, (m + 1) * step)
-            value = jnp.dot(high[at, :], ext, preferred_element_type=F32)
-            value += jnp.dot(low[at, :], ext, preferred_element_type=F32)
-            prod_ref[at, :] = value.astype(BF16)
-
-    if order:
-        place = lax.axis_index("gx")
-        open_side = (place % 2 == 0) & (place > 0)
-
-        @pl.when(open_side)
-        def _():
-            scatter(1, info_ref, a_ref, mine_high, mine_low)
-            product(mine_high, mine_low)
-
-        @pl.when(jnp.logical_not(open_side))
-        def _():
-            product(high_ref.at[1], low_ref.at[1])
-
-    else:
-        product(high_ref.at[0], low_ref.at[0])
+    ext = ext_ref[...]
+    step = prod_ref.shape[0] // 2
+    for m in range(2):
+        at = slice(m * step, (m + 1) * step)
+        value = jnp.dot(high_ref[at, :], ext, preferred_element_type=F32)
+        value += jnp.dot(low_ref[at, :], ext, preferred_element_type=F32)
+        prod_ref[at, :] = value.astype(BF16)
     finish(ownt_ref, prod_ref[...], keep_ref, send_ref)
 
 
@@ -338,13 +322,13 @@
     even = [(i, i + 1) for i in range(0, length - 1, 2)]
     uneven = [(i, i + 1) for i in range(1, length - 1, 2)]
     first = lax.ppermute(first, "gx", even + [(j, i) for i, j in even])
-    split = jax.ShapeDtypeStruct((2, rows * size, count * size), BF16)
-    high, low, second = pl.pallas_call(
+    split = jax.ShapeDtypeStruct((rows * size, count * size), BF16)
+    *laid, second = pl.pallas_call(
         functools.partial(scatter_kernel, False),
-        out_shape=(split, split, packed),
+        out_shape=(split,) * 4 + (packed,),
         in_specs=[VMEM, VMEM, HBM],
-        out_specs=(VMEM, VMEM, HBM),
-        input_output_aliases={2: 2},
+        out_specs=(VMEM,) * 4 + (HBM,),
+        input_output_aliases={2: 4},
         compiler_params=PARAMS,
         cost_estimate=TINY,
         name="scatter",
@@ -370,36 +354,45 @@
         cost_estimate=MEDIUM,
         name="own",
     )(info, ablk, pblk)
-    high, low = pl.pallas_call(
+    laid = pl.pallas_call(
         functools.partial(scatter_kernel, True),
-        out_shape=(split, split),
-        in_specs=[VMEM, VMEM, VMEM, VMEM, VMEM],
-        out_specs=(VMEM, VMEM),
-        input_output_aliases={3: 0, 4: 1},
+        out_shape=(split,) * 4,
+        in_specs=[VMEM] * 7,
+        out_specs=(VMEM,) * 4,
+        input_output_aliases={3: 0, 4: 1, 5: 2, 6: 3},
         compiler_params=PARAMS,
         cost_estimate=TINY,
         name="scatter",
-    )(info, ablk, own_t, high, low)
-
-    def ghost(order, ghosts, *more):
+    )(info, ablk, own_t, *laid)
+
+    def ghost(order, high, low, ghosts):
         return pl.pallas_call(
-            functools.partial(ghost_kernel, order),
+            ghost_kernel,
             out_shape=partial,
-            in_specs=[VMEM] * (4 + len(more)),
+            in_specs=[VMEM] * 4,
             out_specs=(VMEM, VMEM),
             scratch_shapes=[
                 pltpu.VMEM((count * size, width), BF16),
                 pltpu.VMEM((rows * size, width), BF16),
-            ]
-            + [pltpu.VMEM((rows * size, count * size), BF16)] * (2 * order),
+            ],
             compiler_params=PARAMS,
             cost_estimate=LONG,
             name="ghost",
-        )(high, low, ghosts, own_t, *more)
-
-    side_keep, side_send = ghost(0, first)
+        )(high, low, ghosts, own_t)
+
+    side_keep, side_send = ghost(0, *laid[:2], first)
     keep, recv, folds, (side_send,) = folded(keep, send, parts, side_send)
-    last = ghost(1, second, info, ablk, folds)
+    more = pl.pallas_call(
+        second_kernel,
+        out_shape=(split, split),
+        in_specs=[VMEM] * 5,
+        out_specs=(VMEM, VMEM),
+        input_output_aliases={3: 0, 4: 1},
+        compiler_params=PARAMS,
+        cost_estimate=TINY,
+        name="scatter",
+    )(info, ablk, folds, *laid[2:])
+    last = ghost(1, *more, second)
     token = pl.pallas_call(
         gate_kernel,
         out_shape=jax.ShapeDtypeStruct((8, LANES), F32),

time: 23.3 us -> 23.1 us (level)
  starting transfers between devices: 9.59 us -> 9.08 us
  waiting for transfers between devices: 4.06 us -> 4.54 us
    ppermute x6, starting transfers between devices: 5.12 us -> 4.61 us  [swapped(): lax.ppermute(value, axis, [(i, i ^ step) for i in range(length) if i ^ st...]
    ppermute x6, waiting for transfers between devices: 4.02 us -> 4.53 us  [swapped(): lax.ppermute(value, axis, [(i, i ^ step) for i in range(length) if i ^ st...]
    pallas_call x2 -> x3, Pallas kernels: 2.62 us -> 2.61 us  [the longest x2 2.1 us: ghost(): pl.pallas_call(ghost_kernel, out_shape=partial, in_specs=[VMEM] * 4, out_...]
where the time goes in v5:
time: 23.1 us; the launch traced here: 22.9 us
  Pallas kernels  9.09 us (39%)
  starting transfers between devices  9.08 us (39%)
  waiting for transfers between devices  4.54 us (20%)
    ppermute x6, starting transfers between devices, swapped(): lax.ppermute(value, axis, [(i, i ^ step) for i in range(length) if i ^ st...  4.61 us
    ppermute x6, waiting for transfers between devices, swapped(): lax.ppermute(value, axis, [(i, i ^ step) for i in range(length) if i ^ st...  4.53 us
    ppermute x1, starting transfers between devices, body(): second = lax.ppermute(second, 'gx', uneven + [(j, i) for i, j in uneven])  2.92 us
    pallas_call x3, Pallas kernels, written(): pl.pallas_call(functools.partial(write_kernel, order), out_shape=whole, i...  2.24 us
    pallas_call x2, Pallas kernels, ghost(): pl.pallas_call(ghost_kernel, out_shape=partial, in_specs=[VMEM] * 4, out_...  2.1 us
    pallas_call x1, Pallas kernels, body(): pl.pallas_call(pack_kernel, out_shape=(packed, packed, jax.ShapeDtypeStru...  1.76 us
    pallas_call x1, Pallas kernels, body(): pl.pallas_call(functools.partial(own_kernel, parts), out_shape=(jax.Shape...  1.74 us
    ppermute x1, starting transfers between devices, body(): first = lax.ppermute(first, 'gx', even + [(j, i) for i, j in even])  1.56 us
  transfers between devices with their start and end apart: 8, of which 3 were waited for; matrix products, arithmetic and copies ran while one was open for 0% of the time, Pallas kernels for 29%

profile of v5, /device:TPU:24, one launch (start us, length us, event | category | flops | bytes accessed | tf_op | source)
XLA Modules:
  0.0 22.9 jit_solution(4153661651724610021)
XLA Ops:
  0.0 1.8 %pack.1 = (bf16[272,256]{1,0:T(8,128)(2,1)}, bf16[272,256]{1,0:T(8,128)(2,1)}, s32[8,128]{1,0:T(8,128)}) custom-call(s32[8]{0:T(128)} %bitcast.17, s32[4,8]{1,0:T(4,128)} %bitcast.16, s32[7,1,8]{2,1,0:T(1,128)} %bitcast.15, s32[8]{0:T(128)} %bitcast.18, bf16[8,64,256]{2,1,0:T(8,128)(2,1)} %bitcast.13), custom_call_target="tpu_custom_call" | custom-call | flops 10000000000 | bytes 1000000 | tf_op jit(solution)/shard_map/pack/pallas_call | solution.py:303
  1.8 1.6 %collective-permute-start.1 = (bf16[272,256]{1,0:T(8,128)(2,1)}, bf16[272,256]{1,0:T(8,128)(2,1)S(1)}, u32[]{:S(2)}, u32[]{:S(2)}) collective-permute-start(bf16[272,256]{1,0:T(8,128)(2,1)} %get-tuple-element.44), channel_id=1, source_target_pairs={{0,4},{8,12},{16,20},{24,28},{4,0},{12,8},{20,16},{28,24},{1,5},{9... | collective-permute-start | bytes 417800 | tf_op jit(solution)/shard_map/ppermute | solution.py:324
  3.4 2.9 %collective-permute-start.2 = (bf16[272,256]{1,0:T(8,128)(2,1)}, bf16[272,256]{1,0:T(8,128)(2,1)S(1)}, u32[]{:S(2)}, u32[]{:S(2)}) collective-permute-start(bf16[272,256]{1,0:T(8,128)(2,1)} %get-tuple-element.51), channel_id=1, source_target_pairs={{4,8},{12,16},{20,24},{8,4},{16,12},{24,20},{5,9},{13,17},{21,25},... | collective-permute-start | bytes 417800 | tf_op jit(solution)/shard_map/ppermute | solution.py:336
  6.3 1.7 %own.1 = (bf16[512,512]{1,0:T(8,128)(2,1)S(1)}, f32[2,128,512]{2,1,0:T(8,128)S(1)}, bf16[2,128,512]{2,1,0:T(8,128)(2,1)S(1)}) custom-call(s32[8,128]{1,0:T(8,128)S(1)} %copy-done.1, bf16[8,64,448]{2,1,0:T(8,128)(2,1)S(1)} %bitcast.10, bf16[8,64,256]{2,1,0:T(8,128)(2,1)S(1)} %bitcast.14), custom_call_target="tpu_custom_call" | custom-call | flops 1000000000 | bytes 1000000 | tf_op jit(solution)/shard_map/own/pallas_call | solution.py:342
  8.0 0.1 collective-permute-start
  8.1 0.5 %scatter.4 = (bf16[512,256]{1,0:T(8,128)(2,1)S(1)}, bf16[512,256]{1,0:T(8,128)(2,1)S(1)}, bf16[512,256]{1,0:T(8,128)(2,1)S(1)}, bf16[512,256]{1,0:T(8,128)(2,1)S(1)}) custom-call(s32[8,128]{1,0:T(8,128)S(1)} %copy-done.1, bf16[8,64,448]{2,1,0:T(8,128)(2,1)S(1)} %bitcast.11, ...), custom_call_target="tpu_custom_call", output_to_operand_aliasing={{0}: (3, {}), {1}: (4, {}), {2}: (5, {}), {3}: (6, {})} | custom-call | flops 1000000 | bytes 1000000 | tf_op jit(solution)/shard_map/scatter/pallas_call | solution.py:357
  8.7 0.0 collective-permute-done.1.in_ref
  8.7 1.0 %ghost.2 = (f32[2,128,512]{2,1,0:T(8,128)S(1)}, bf16[2,128,512]{2,1,0:T(8,128)(2,1)S(1)}) custom-call(bf16[512,256]{1,0:T(8,128)(2,1)S(1)} %get-tuple-element.42.high_ref, bf16[512,256]{1,0:T(8,128)(2,1)S(1)} %get-tuple-element.43.low_ref, bf16[272,256]{1,0:T(8,128)(2,1)S(1)} %collective-permute-done.1.in_ref, ...), custom_call_target="tpu_custom_call" | custom-call | flops 10000000000 | bytes 1000000 | tf_op jit(solution)/shard_map/ghost/pallas_call | solution.py:369
  9.7 0.1 fold.3
  9.8 1.6 %collective-permute-start.4 = (bf16[1,128,512]{2,1,0:T(8,128)(2,1)S(1)}, bf16[1,128,512]{2,1,0:T(8,128)(2,1)S(1)}, u32[]{:S(2)}, u32[]{:S(2)}) collective-permute-start(bf16[1,128,512]{2,1,0:T(8,128)(2,1)S(1)} %get-tuple-element.54), channel_id=1, source_target_pairs={{0,2},{1,3},{2,0},{3,1},{4,6},{5,7},{6,4},{7,5},{8,10},{9,11},{10,... | collective-permute-start | bytes 393224 | tf_op jit(solution)/shard_map/ppermute | solution.py:238
  11.4 0.2 collective-permute-start.6
  11.6 0.5 %scatter.5 = (bf16[512,256]{1,0:T(8,128)(2,1)S(1)}, bf16[512,256]{1,0:T(8,128)(2,1)S(1)}) custom-call(s32[8,128]{1,0:T(8,128)S(1)} %copy-done.1, bf16[8,64,448]{2,1,0:T(8,128)(2,1)S(1)} %bitcast.12, f32[1,128,512]{2,1,0:T(8,128)S(1)} %get-tuple-element.46.after.keep_ref, ...), custom_call_target="tpu_custom_call", output_to_operand_aliasing={{0}: (3, {}), {1}: (4, {})} | custom-call | flops 1000000 | bytes 1000000 | tf_op jit(solution)/shard_map/scatter/pallas_call | solution.py:385
  12.1 1.0 %ghost.3 = (f32[2,128,512]{2,1,0:T(8,128)S(1)}, bf16[2,128,512]{2,1,0:T(8,128)(2,1)S(1)}) custom-call(bf16[512,256]{1,0:T(8,128)(2,1)S(1)} %get-tuple-element.49.high_ref, bf16[512,256]{1,0:T(8,128)(2,1)S(1)} %get-tuple-element.50.low_ref, bf16[272,256]{1,0:T(8,128)(2,1)S(1)} %collective-permute-done.2.in_ref, ...), custom_call_target="tpu_custom_call" | custom-call | flops 10000000000 | bytes 1000000 | tf_op jit(solution)/shard_map/ghost/pallas_call | solution.py:369
  13.2 0.4 %collective-permute-start.3 = (bf16[2,128,512]{2,1,0:T(8,128)(2,1)S(1)}, bf16[2,128,512]{2,1,0:T(8,128)(2,1)S(1)}, u32[]{:S(2)}, u32[]{:S(2)}) collective-permute-start(bf16[2,128,512]{2,1,0:T(8,128)(2,1)S(1)} %get-tuple-element.53), channel_id=1, source_target_pairs={{0,1},{1,0},{2,3},{3,2},{4,5},{5,4},{6,7},{7,6},{8,9},{9,8},{10,11... | collective-permute-start | bytes 786440 | tf_op jit(solution)/shard_map/ppermute | solution.py:238
  13.6 0.1 fold.5
  13.6 0.8 %collective-permute-start.7 = (bf16[1,128,512]{2,1,0:T(8,128)(2,1)S(1)}, bf16[1,128,512]{2,1,0:T(8,128)(2,1)S(1)}, u32[]{:S(2)}, u32[]{:S(2)}) collective-permute-start(bf16[1,128,512]{2,1,0:T(8,128)(2,1)S(1)} %get-tuple-element.60), channel_id=1, source_target_pairs={{0,2},{1,3},{2,0},{3,1},{4,6},{5,7},{6,4},{7,5},{8,10},{9,11},{10,... | collective-permute-start | bytes 393224 | tf_op jit(solution)/shard_map/ppermute | solution.py:238
  14.4 1.3 %collective-permute-done.4.recv_ref = bf16[1,128,512]{2,1,0:T(8,128)(2,1)S(1)} collective-permute-done((bf16[1,128,512]{2,1,0:T(8,128)(2,1)S(1)}, bf16[1,128,512]{2,1,0:T(8,128)(2,1)S(1)}, u32[]{:S(2)}, u32[]{:S(2)}) %collective-permute-start.4) | collective-permute-done | bytes 131104 | tf_op jit(solution)/shard_map/ppermute | solution.py:238
  15.8 0.1 fold.4
  15.8 1.6 %collective-permute-start.5 = (bf16[1,128,512]{2,1,0:T(8,128)(2,1)S(1)}, bf16[1,128,512]{2,1,0:T(8,128)(2,1)S(1)}, u32[]{:S(2)}, u32[]{:S(2)}) collective-permute-start(bf16[1,128,512]{2,1,0:T(8,128)(2,1)S(1)} %get-tuple-element.56), channel_id=1, source_target_pairs={{0,2},{1,3},{2,0},{3,1},{4,6},{5,7},{6,4},{7,5},{8,10},{9,11},{10,... | collective-permute-start | bytes 393224 | tf_op jit(solution)/shard_map/ppermute | solution.py:238
  17.4 0.7 %write.3.refs_0_ = f32[128,1536]{1,0:T(8,128)} custom-call(f32[1,128,512]{2,1,0:T(8,128)S(1)} %get-tuple-element.46.after.keep_ref, bf16[1,128,512]{2,1,0:T(8,128)(2,1)S(1)} %collective-permute-done.4.recv_ref), custom_call_target="tpu_custom_call" | custom-call | flops 100000000 | bytes 1000000 | tf_op jit(solution)/shard_map/write/pallas_call | solution.py:273
  18.1 1.9 %collective-permute-done.7.recv_ref = bf16[1,128,512]{2,1,0:T(8,128)(2,1)S(1)} collective-permute-done((bf16[1,128,512]{2,1,0:T(8,128)(2,1)S(1)}, bf16[1,128,512]{2,1,0:T(8,128)(2,1)S(1)}, u32[]{:S(2)}, u32[]{:S(2)}) %collective-permute-start.7) | collective-permute-done | bytes 131104 | tf_op jit(solution)/shard_map/ppermute | solution.py:238
  20.0 0.8 %write.4.refs_0_ = f32[128,1536]{1,0:T(8,128)} custom-call(f32[1,128,512]{2,1,0:T(8,128)S(1)} %get-tuple-element.59.keep_ref, bf16[1,128,512]{2,1,0:T(8,128)(2,1)S(1)} %collective-permute-done.7.recv_ref, f32[128,1536]{1,0:T(8,128)} %write.3.refs_0_), custom_call_target="tpu_custom_call", output_to_operand_aliasing={{}: (2, {})} | custom-call | flops 100000000 | bytes 1000000 | tf_op jit(solution)/shard_map/write/pallas_call | solution.py:273
  20.8 1.3 %collective-permute-done.5.recv_ref = bf16[1,128,512]{2,1,0:T(8,128)(2,1)S(1)} collective-permute-done((bf16[1,128,512]{2,1,0:T(8,128)(2,1)S(1)}, bf16[1,128,512]{2,1,0:T(8,128)(2,1)S(1)}, u32[]{:S(2)}, u32[]{:S(2)}) %collective-permute-start.5) | collective-permute-done | bytes 131104 | tf_op jit(solution)/shard_map/ppermute | solution.py:238
  22.1 0.8 %write.5 = f32[128,1536]{1,0:T(8,128)} custom-call(f32[1,128,512]{2,1,0:T(8,128)S(1)} %get-tuple-element.55.keep_ref, bf16[1,128,512]{2,1,0:T(8,128)(2,1)S(1)} %collective-permute-done.5.recv_ref, f32[128,1536]{1,0:T(8,128)} %write.4.refs_0_), custom_call_target="tpu_custom_call", output_to_operand_aliasing={{}: (2, {})} | custom-call | flops 100000000 | bytes 1000000 | tf_op jit(solution)/shard_map/write/pallas_call | solution.py:273
  (12 shorter events, 0.0 us)
Async XLA Ops:
  0.0 3.3 %copy-start = (bf16[1,8,64,448]{3,2,1,0:T(8,128)(2,1)S(1)}, bf16[1,8,64,448]{3,2,1,0:T(8,128)(2,1)}, u32[]{:S(2)}) copy-start(bf16[1,8,64,448]{3,2,1,0:T(8,128)(2,1)} %param.6) | copy-start | bytes 1376260
  1.8 1.6 %copy-start.1 = (s32[8,128]{1,0:T(8,128)S(1)}, s32[8,128]{1,0:T(8,128)}, u32[]{:S(2)}) copy-start(s32[8,128]{1,0:T(8,128)} %get-tuple-element.33.info_ref) | copy-start | bytes 12292
  1.8 6.9 %collective-permute-start.1 = (bf16[272,256]{1,0:T(8,128)(2,1)}, bf16[272,256]{1,0:T(8,128)(2,1)S(1)}, u32[]{:S(2)}, u32[]{:S(2)}) collective-permute-start(bf16[272,256]{1,0:T(8,128)(2,1)} %get-tuple-element.44), channel_id=1, source_target_pairs={{0,4},{8,12},{16,20},{24,28},{4,0},{12,8},{20,16},{28,24},{1,5},{9... | collective-permute-start | bytes 417800 | tf_op jit(solution)/shard_map/ppermute | solution.py:324
  3.3 2.9 %copy-start.2 = (bf16[1,8,64,256]{3,2,1,0:T(8,128)(2,1)S(1)}, bf16[1,8,64,256]{3,2,1,0:T(8,128)(2,1)}, u32[]{:S(2)}) copy-start(bf16[1,8,64,256]{3,2,1,0:T(8,128)(2,1)} %param.9) | copy-start | bytes 786436
  3.4 8.8 %collective-permute-start.2 = (bf16[272,256]{1,0:T(8,128)(2,1)}, bf16[272,256]{1,0:T(8,128)(2,1)S(1)}, u32[]{:S(2)}, u32[]{:S(2)}) collective-permute-start(bf16[272,256]{1,0:T(8,128)(2,1)} %get-tuple-element.51), channel_id=1, source_target_pairs={{4,8},{12,16},{20,24},{8,4},{16,12},{24,20},{5,9},{13,17},{21,25},... | collective-permute-start | bytes 417800 | tf_op jit(solution)/shard_map/ppermute | solution.py:336
  8.0 1.7 %collective-permute-start = (bf16[2,128,512]{2,1,0:T(8,128)(2,1)S(1)}, bf16[2,128,512]{2,1,0:T(8,128)(2,1)S(1)}, u32[]{:S(2)}, u32[]{:S(2)}) collective-permute-start(bf16[2,128,512]{2,1,0:T(8,128)(2,1)S(1)} %get-tuple-element.35), channel_id=1, source_target_pairs={{0,1},{1,0},{2,3},{3,2},{4,5},{5,4},{6,7},{7,6},{8,9},{9,8},{10,11... | collective-permute-start | bytes 786440 | tf_op jit(solution)/shard_map/ppermute | solution.py:238
  9.8 5.9 %collective-permute-start.4 = (bf16[1,128,512]{2,1,0:T(8,128)(2,1)S(1)}, bf16[1,128,512]{2,1,0:T(8,128)(2,1)S(1)}, u32[]{:S(2)}, u32[]{:S(2)}) collective-permute-start(bf16[1,128,512]{2,1,0:T(8,128)(2,1)S(1)} %get-tuple-element.54), channel_id=1, source_target_pairs={{0,2},{1,3},{2,0},{3,1},{4,6},{5,7},{6,4},{7,5},{8,10},{9,11},{10,... | collective-permute-start | bytes 393224 | tf_op jit(solution)/shard_map/ppermute | solution.py:238
  11.4 2.2 %collective-permute-start.6 = (bf16[2,128,512]{2,1,0:T(8,128)(2,1)S(1)}, bf16[2,128,512]{2,1,0:T(8,128)(2,1)S(1)}, u32[]{:S(2)}, u32[]{:S(2)}) collective-permute-start(bf16[2,128,512]{2,1,0:T(8,128)(2,1)S(1)} %get-tuple-element.58), channel_id=1, source_target_pairs={{0,1},{1,0},{2,3},{3,2},{4,5},{5,4},{6,7},{7,6},{8,9},{9,8},{10,11... | collective-permute-start | bytes 786440 | tf_op jit(solution)/shard_map/ppermute | solution.py:238
  13.2 2.6 %collective-permute-start.3 = (bf16[2,128,512]{2,1,0:T(8,128)(2,1)S(1)}, bf16[2,128,512]{2,1,0:T(8,128)(2,1)S(1)}, u32[]{:S(2)}, u32[]{:S(2)}) collective-permute-start(bf16[2,128,512]{2,1,0:T(8,128)(2,1)S(1)} %get-tuple-element.53), channel_id=1, source_target_pairs={{0,1},{1,0},{2,3},{3,2},{4,5},{5,4},{6,7},{7,6},{8,9},{9,8},{10,11... | collective-permute-start | bytes 786440 | tf_op jit(solution)/shard_map/ppermute | solution.py:238
  13.6 6.4 %collective-permute-start.7 = (bf16[1,128,512]{2,1,0:T(8,128)(2,1)S(1)}, bf16[1,128,512]{2,1,0:T(8,128)(2,1)S(1)}, u32[]{:S(2)}, u32[]{:S(2)}) collective-permute-start(bf16[1,128,512]{2,1,0:T(8,128)(2,1)S(1)} %get-tuple-element.60), channel_id=1, source_target_pairs={{0,2},{1,3},{2,0},{3,1},{4,6},{5,7},{6,4},{7,5},{8,10},{9,11},{10,... | collective-permute-start | bytes 393224 | tf_op jit(solution)/shard_map/ppermute | solution.py:238
  15.8 6.3 %collective-permute-start.5 = (bf16[1,128,512]{2,1,0:T(8,128)(2,1)S(1)}, bf16[1,128,512]{2,1,0:T(8,128)(2,1)S(1)}, u32[]{:S(2)}, u32[]{:S(2)}) collective-permute-start(bf16[1,128,512]{2,1,0:T(8,128)(2,1)S(1)} %get-tuple-element.56), channel_id=1, source_target_pairs={{0,2},{1,3},{2,0},{3,1},{4,6},{5,7},{6,4},{7,5},{8,10},{9,11},{10,... | collective-permute-start | bytes 393224 | tf_op jit(solution)/shard_map/ppermute | solution.py:238

commit v6 on v5

--- a/solution.py
+++ b/solution.py
@@ -11,6 +11,7 @@
 KS = 3
 NCOL = 8
 LANES = 128
+SPLIT = 2
 WIDE = 256
 
 F32 = jnp.float32
@@ -65,10 +66,12 @@
         prod_ref[n * size : (n + 1) * size, :] = value.astype(BF16)
 
 
-def finish(ownt_ref, prod, keep_ref, send_ref):
+def finish(ownt_ref, prod, keep_ref, *send_refs):
     rows = ownt_ref.shape[0] // 2
-    sent = jnp.dot(ownt_ref[rows:, :], prod, preferred_element_type=F32)
-    send_ref[...] = sent.astype(BF16).reshape(send_ref.shape)
+    sent = jnp.dot(ownt_ref[rows:, :], prod, preferred_element_type=F32).astype(BF16)
+    wide = sent.shape[1] // len(send_refs)
+    for i, send_ref in enumerate(send_refs):
+        send_ref[...] = sent[:, i * wide : (i + 1) * wide].reshape(send_ref.shape)
     kept = jnp.dot(ownt_ref[:rows, :], prod, preferred_element_type=F32)
     keep_ref[...] = kept.reshape(keep_ref.shape)
 
@@ -181,7 +184,8 @@
     pl.when((place % 2 == 0) & (place > 0))(lambda: scatter(1, info_ref, a_ref, *refs[-2:]))
 
 
-def ghost_kernel(high_ref, low_ref, in_ref, ownt_ref, keep_ref, send_ref, ext_ref, prod_ref):
+def ghost_kernel(high_ref, low_ref, in_ref, ownt_ref, keep_ref, *refs):
+    *send_refs, ext_ref, prod_ref = refs
     width = ownt_ref.shape[0]
     size = width // NCOL
     slots = in_ref.shape[1] // size
@@ -200,16 +204,24 @@
         value = jnp.dot(high_ref[at, :], ext, preferred_element_type=F32)
         value += jnp.dot(low_ref[at, :], ext, preferred_element_type=F32)
         prod_ref[at, :] = value.astype(BF16)
-    finish(ownt_ref, prod_ref[...], keep_ref, send_ref)
-
-
-def fold_kernel(stage, count, keep_ref, recv_ref, *refs):
-    next_ref, send_ref = refs[count : count + 2]
+    finish(ownt_ref, prod_ref[...], keep_ref, *send_refs)
+
+
+def fold_kernel(stage, pieces, count, keep_ref, *refs):
+    recv_refs = refs[:pieces]
+    next_ref, send_ref = refs[pieces + count : pieces + count + 2]
     bit = (lax.axis_index("gy") >> stage) % 2
-    for i in range(next_ref.shape[0]):
-        mine, other = 2 * i + bit, 2 * i + 1 - bit
-        send_ref[i] = (keep_ref[other] + recv_ref[other].astype(F32)).astype(BF16)
-        next_ref[i] = keep_ref[mine] + recv_ref[mine].astype(F32)
+    wide = keep_ref.shape[2] // pieces
+    share = keep_ref.shape[1]
+    if send_ref.shape[1] > share:
+        send_ref[:, share:, :] = jnp.zeros_like(send_ref[:, share:, :])
+    for c, recv_ref in enumerate(recv_refs):
+        at = slice(c * wide, (c + 1) * wide)
+        for i in range(next_ref.shape[0]):
+            mine, other = 2 * i + bit, 2 * i + 1 - bit
+            sent = keep_ref[other, :, at] + recv_ref[other].astype(F32)
+            send_ref[i, : sent.shape[0], at] = sent.astype(BF16)
+            next_ref[i, :, at] = keep_ref[mine, :, at] + recv_ref[mine].astype(F32)
 
 
 def write_kernel(order, keep_ref, recv_ref, *refs):
@@ -229,51 +241,48 @@
         copy.wait()
 
 
-def gate_kernel(recv_ref, token_ref):
-    token_ref[...] = jnp.zeros(token_ref.shape, F32)
-
-
 def swapped(value, axis, step):
     length = lax.axis_size(axis)
     return lax.ppermute(value, axis, [(i, i ^ step) for i in range(length) if i ^ step < length])
 
 
-def folded(keep, send, parts, *passed):
+def folded(keep, sends, parts, *passed, extra=0):
     left, share, width = keep.shape
     stage = 0
     later = ()
     while left > 1:
-        recv = swapped(send, "gy", 1 << stage)
+        recvs = [swapped(send, "gy", 1 << stage) for send in sends]
         stage += 1
         left //= 2
         through = passed if stage == 1 else ()
         count = len(through)
         keep, send, *through = pl.pallas_call(
-            functools.partial(fold_kernel, stage, count),
+            functools.partial(fold_kernel, stage, len(recvs), count),
             out_shape=(
                 jax.ShapeDtypeStruct((left, share, width), F32),
-                jax.ShapeDtypeStruct((left, share, width), BF16),
+                jax.ShapeDtypeStruct((left, share + (extra if left == 1 else 0), width), BF16),
             )
             + tuple(jax.ShapeDtypeStruct(value.shape, value.dtype) for value in through),
-            in_specs=[VMEM] * (2 + count),
+            in_specs=[VMEM] * (1 + len(recvs) + count),
             out_specs=(VMEM,) * (2 + count),
-            input_output_aliases={2 + i: 2 + i for i in range(count)},
+            input_output_aliases={1 + len(recvs) + i: 2 + i for i in range(count)},
             compiler_params=PARAMS,
             name="fold",
-        )(keep, recv, *through)
+        )(keep, *recvs, *through)
+        sends = [send]
         if stage == 1:
             later, folds = through, keep
-    return keep, swapped(send, "gy", 1 << stage), folds, later
-
-
-def written(order, keep, recv, result):
+    return keep, swapped(sends[0], "gy", 1 << stage), folds, later
+
+
+def written(order, keep, recv, result, *after):
     share, width = keep.shape[1:]
     start = order is None
     whole = jax.ShapeDtypeStruct((share, 3 * width), F32)
     return pl.pallas_call(
         functools.partial(write_kernel, order),
         out_shape=whole,
-        in_specs=[VMEM, VMEM] if start else [VMEM, VMEM, HBM],
+        in_specs=[VMEM, VMEM] + ([VMEM] * len(after) if start else [HBM]),
         out_specs=HBM,
         input_output_aliases={} if start else {2: 0},
         scratch_shapes=[
@@ -281,9 +290,9 @@
             pltpu.SemaphoreType.DMA((max(1, min(4, share // 16)),)),
         ],
         compiler_params=PARAMS,
-        cost_estimate=SHORT,
+        cost_estimate=TINY if start else LONG,
         name="write",
-    )(keep, recv, *([] if start else [result]))
+    )(keep, recv, *(after if start else [result]))
 
 
 def body(a_blocks, a_cols, mushy, p_blocks, p_cols, send_rows):
@@ -365,12 +374,14 @@
         name="scatter",
     )(info, ablk, own_t, *laid)
 
+    small = jax.ShapeDtypeStruct((parts // 2, share, width // SPLIT), BF16)
+
     def ghost(order, high, low, ghosts):
         return pl.pallas_call(
             ghost_kernel,
-            out_shape=partial,
+            out_shape=(partial[0],) + (small,) * SPLIT if order else partial,
             in_specs=[VMEM] * 4,
-            out_specs=(VMEM, VMEM),
+            out_specs=(VMEM,) * (1 + (SPLIT if order else 1)),
             scratch_shapes=[
                 pltpu.VMEM((count * size, width), BF16),
                 pltpu.VMEM((rows * size, width), BF16),
@@ -381,7 +392,7 @@
         )(high, low, ghosts, own_t)
 
     side_keep, side_send = ghost(0, *laid[:2], first)
-    keep, recv, folds, (side_send,) = folded(keep, send, parts, side_send)
+    keep, recv, folds, (side_send,) = folded(keep, [send], parts, side_send, extra=16)
     more = pl.pallas_call(
         second_kernel,
         out_shape=(split, split),
@@ -392,19 +403,12 @@
         cost_estimate=TINY,
         name="scatter",
     )(info, ablk, folds, *laid[2:])
-    last = ghost(1, *more, second)
-    token = pl.pallas_call(
-        gate_kernel,
-        out_shape=jax.ShapeDtypeStruct((8, LANES), F32),
-        in_specs=[HBM],
-        out_specs=VMEM,
-        compiler_params=PARAMS,
-        cost_estimate=LONG,
-        name="gate",
-    )(recv)
-    sides = [folded(side_keep, side_send, parts), folded(*last, parts, token)]
-    result = written(None, keep, recv, None)
-    for order, (keep, recv, folds, later) in enumerate(sides):
+    last_keep, *last_sends = ghost(1, *more, second)
+    side_keep, side_recv, _, _ = folded(side_keep, [side_send], parts)
+    last_keep, last_recv, _, (side_keep,) = folded(last_keep, last_sends, parts, side_keep)
+    sides = [(side_keep, side_recv), (last_keep, last_recv)]
+    result = written(None, keep, recv, None, last_keep)
+    for order, (keep, recv) in enumerate(sides):
         result = written(order, keep, recv, result)
     return result[None]
 

time: 23.1 us -> 23.5 us (1.017)
  waiting for transfers between devices: 4.54 us -> 4.88 us
    ppermute x6 -> x7, waiting for transfers between devices: 4.53 us -> 4.87 us  [swapped(): lax.ppermute(value, axis, [(i, i ^ step) for i in range(length) if i ^ st...]
    ppermute x6 -> x7, starting transfers between devices: 4.61 us -> 4.58 us  [swapped(): lax.ppermute(value, axis, [(i, i ^ step) for i in range(length) if i ^ st...]
    pallas_call x6 -> x5, Pallas kernels: 2.28 us -> 2.27 us  [the longest x2 2.1 us: ghost(): pl.pallas_call(ghost_kernel, out_shape=(partial[0],) + (small,) * SPLIT i...]
  transfers between devices with their start and end apart: 8 -> 9, of which waited for: 3 -> 3; matrix products, arithmetic and copies ran while one was open for 0% -> 0% of each run, Pallas kernels for 29% -> 28%
where the time goes in v6:
time: 23.5 us; the launch traced here: 23.2 us
  Pallas kernels  9.08 us (39%)
  starting transfers between devices  9.04 us (38%)
  waiting for transfers between devices  4.88 us (21%)
    ppermute x7, waiting for transfers between devices, swapped(): lax.ppermute(value, axis, [(i, i ^ step) for i in range(length) if i ^ st...  4.87 us
    ppermute x7, starting transfers between devices, swapped(): lax.ppermute(value, axis, [(i, i ^ step) for i in range(length) if i ^ st...  4.58 us
    ppermute x1, starting transfers between devices, body(): second = lax.ppermute(second, 'gx', uneven + [(j, i) for i, j in uneven])  2.91 us
    pallas_call x3, Pallas kernels, written(): pl.pallas_call(functools.partial(write_kernel, order), out_shape=whole, i...  2.24 us
    pallas_call x2, Pallas kernels, ghost(): pl.pallas_call(ghost_kernel, out_shape=(partial[0],) + (small,) * SPLIT i...  2.1 us
    pallas_call x1, Pallas kernels, body(): pl.pallas_call(pack_kernel, out_shape=(packed, packed, jax.ShapeDtypeStru...  1.77 us
    pallas_call x1, Pallas kernels, body(): pl.pallas_call(functools.partial(own_kernel, parts), out_shape=(jax.Shape...  1.75 us
    ppermute x1, starting transfers between devices, body(): first = lax.ppermute(first, 'gx', even + [(j, i) for i, j in even])  1.56 us
  transfers between devices with their start and end apart: 9, of which 3 were waited for; matrix products, arithmetic and copies ran while one was open for 0% of the time, Pallas kernels for 28%

profile of v6, /device:TPU:24, one launch (start us, length us, event | category | flops | bytes accessed | tf_op | source)
XLA Modules:
  0.0 23.2 jit_solution(15669146454071074883)
XLA Ops:
  0.0 1.8 %pack.1 = (bf16[272,256]{1,0:T(8,128)(2,1)}, bf16[272,256]{1,0:T(8,128)(2,1)}, s32[8,128]{1,0:T(8,128)}) custom-call(s32[8]{0:T(128)} %bitcast.17, s32[4,8]{1,0:T(4,128)} %bitcast.16, s32[7,1,8]{2,1,0:T(1,128)} %bitcast.15, s32[8]{0:T(128)} %bitcast.18, bf16[8,64,256]{2,1,0:T(8,128)(2,1)} %bitcast.13), custom_call_target="tpu_custom_call" | custom-call | flops 10000000000 | bytes 1000000 | tf_op jit(solution)/shard_map/pack/pallas_call | solution.py:312
  1.8 1.6 %collective-permute-start.1 = (bf16[272,256]{1,0:T(8,128)(2,1)}, bf16[272,256]{1,0:T(8,128)(2,1)S(1)}, u32[]{:S(2)}, u32[]{:S(2)}) collective-permute-start(bf16[272,256]{1,0:T(8,128)(2,1)} %get-tuple-element.46), channel_id=1, source_target_pairs={{0,4},{8,12},{16,20},{24,28},{4,0},{12,8},{20,16},{28,24},{1,5},{9... | collective-permute-start | bytes 417800 | tf_op jit(solution)/shard_map/ppermute | solution.py:333
  3.4 2.9 %collective-permute-start.2 = (bf16[272,256]{1,0:T(8,128)(2,1)}, bf16[272,256]{1,0:T(8,128)(2,1)S(1)}, u32[]{:S(2)}, u32[]{:S(2)}) collective-permute-start(bf16[272,256]{1,0:T(8,128)(2,1)} %get-tuple-element.53), channel_id=1, source_target_pairs={{4,8},{12,16},{20,24},{8,4},{16,12},{24,20},{5,9},{13,17},{21,25},... | collective-permute-start | bytes 417800 | tf_op jit(solution)/shard_map/ppermute | solution.py:345
  6.3 1.7 %own.1 = (bf16[512,512]{1,0:T(8,128)(2,1)S(1)}, f32[2,128,512]{2,1,0:T(8,128)S(1)}, bf16[2,128,512]{2,1,0:T(8,128)(2,1)S(1)}) custom-call(s32[8,128]{1,0:T(8,128)S(1)} %copy-done.1, bf16[8,64,448]{2,1,0:T(8,128)(2,1)S(1)} %bitcast.10, bf16[8,64,256]{2,1,0:T(8,128)(2,1)S(1)} %bitcast.14), custom_call_target="tpu_custom_call" | custom-call | flops 1000000000 | bytes 1000000 | tf_op jit(solution)/shard_map/own/pallas_call | solution.py:351
  8.0 0.1 collective-permute-start
  8.1 0.5 %scatter.4 = (bf16[512,256]{1,0:T(8,128)(2,1)S(1)}, bf16[512,256]{1,0:T(8,128)(2,1)S(1)}, bf16[512,256]{1,0:T(8,128)(2,1)S(1)}, bf16[512,256]{1,0:T(8,128)(2,1)S(1)}) custom-call(s32[8,128]{1,0:T(8,128)S(1)} %copy-done.1, bf16[8,64,448]{2,1,0:T(8,128)(2,1)S(1)} %bitcast.11, ...), custom_call_target="tpu_custom_call", output_to_operand_aliasing={{0}: (3, {}), {1}: (4, {}), {2}: (5, {}), {3}: (6, {})} | custom-call | flops 1000000 | bytes 1000000 | tf_op jit(solution)/shard_map/scatter/pallas_call | solution.py:366
  8.7 0.0 collective-permute-done.1.in_ref
  8.7 1.0 %ghost.2 = (f32[2,128,512]{2,1,0:T(8,128)S(1)}, bf16[2,128,512]{2,1,0:T(8,128)(2,1)S(1)}) custom-call(bf16[512,256]{1,0:T(8,128)(2,1)S(1)} %get-tuple-element.44.high_ref, bf16[512,256]{1,0:T(8,128)(2,1)S(1)} %get-tuple-element.45.low_ref, bf16[272,256]{1,0:T(8,128)(2,1)S(1)} %collective-permute-done.1.in_ref, ...), custom_call_target="tpu_custom_call" | custom-call | flops 10000000000 | bytes 1000000 | tf_op jit(solution)/shard_map/ghost/pallas_call | solution.py:380
  9.7 0.1 fold.3
  9.8 1.6 %collective-permute-start.8 = (bf16[1,144,512]{2,1,0:T(8,128)(2,1)S(1)}, bf16[1,144,512]{2,1,0:T(8,128)(2,1)S(1)}, u32[]{:S(2)}, u32[]{:S(2)}) collective-permute-start(bf16[1,144,512]{2,1,0:T(8,128)(2,1)S(1)} %get-tuple-element.64), channel_id=1, source_target_pairs={{0,2},{1,3},{2,0},{3,1},{4,6},{5,7},{6,4},{7,5},{8,10},{9,11},{10,... | collective-permute-start | bytes 442376 | tf_op jit(solution)/shard_map/ppermute | solution.py:246
  11.4 0.2 collective-permute-start.5
  11.6 0.5 %scatter.5 = (bf16[512,256]{1,0:T(8,128)(2,1)S(1)}, bf16[512,256]{1,0:T(8,128)(2,1)S(1)}) custom-call(s32[8,128]{1,0:T(8,128)S(1)} %copy-done.1, bf16[8,64,448]{2,1,0:T(8,128)(2,1)S(1)} %bitcast.12, f32[1,128,512]{2,1,0:T(8,128)S(1)} %get-tuple-element.48.after.keep_ref, ...), custom_call_target="tpu_custom_call", output_to_operand_aliasing={{0}: (3, {}), {1}: (4, {})} | custom-call | flops 1000000 | bytes 1000000 | tf_op jit(solution)/shard_map/scatter/pallas_call | solution.py:396
  12.1 1.0 %ghost.3 = (f32[2,128,512]{2,1,0:T(8,128)S(1)}, bf16[2,128,256]{2,1,0:T(8,128)(2,1)S(1)}, bf16[2,128,256]{2,1,0:T(8,128)(2,1)S(1)}) custom-call(bf16[512,256]{1,0:T(8,128)(2,1)S(1)} %get-tuple-element.51.high_ref, bf16[512,256]{1,0:T(8,128)(2,1)S(1)} %get-tuple-element.52.low_ref, bf16[272,256]{1,0:T(8,128)(2,1)S(1)} %collective-permute-done.2.in_ref, ...), custom_call_target="tpu_custom_call" | custom-call | flops 10000000000 | bytes 1000000 | tf_op jit(solution)/shard_map/ghost/pallas_call | solution.py:380
  13.2 0.4 %collective-permute-start.3 = (bf16[2,128,256]{2,1,0:T(8,128)(2,1)S(1)}, bf16[2,128,256]{2,1,0:T(8,128)(2,1)S(1)}, u32[]{:S(2)}, u32[]{:S(2)}) collective-permute-start(bf16[2,128,256]{2,1,0:T(8,128)(2,1)S(1)} %get-tuple-element.55), channel_id=1, source_target_pairs={{0,1},{1,0},{2,3},{3,2},{4,5},{5,4},{6,7},{7,6},{8,9},{9,8},{10,11... | collective-permute-start | bytes 393224 | tf_op jit(solution)/shard_map/ppermute | solution.py:246
  13.6 0.2 collective-permute-start.4
  13.8 0.1 fold.4
  13.8 1.1 %collective-permute-start.7 = (bf16[1,128,512]{2,1,0:T(8,128)(2,1)S(1)}, bf16[1,128,512]{2,1,0:T(8,128)(2,1)S(1)}, u32[]{:S(2)}, u32[]{:S(2)}) collective-permute-start(bf16[1,128,512]{2,1,0:T(8,128)(2,1)S(1)} %get-tuple-element.63), channel_id=1, source_target_pairs={{0,2},{1,3},{2,0},{3,1},{4,6},{5,7},{6,4},{7,5},{8,10},{9,11},{10,... | collective-permute-start | bytes 393224 | tf_op jit(solution)/shard_map/ppermute | solution.py:246
  15.0 1.1 %collective-permute-start.6 = (bf16[1,128,512]{2,1,0:T(8,128)(2,1)S(1)}, bf16[1,128,512]{2,1,0:T(8,128)(2,1)S(1)}, u32[]{:S(2)}, u32[]{:S(2)}) collective-permute-start(bf16[1,128,512]{2,1,0:T(8,128)(2,1)S(1)} %get-tuple-element.61), channel_id=1, source_target_pairs={{0,2},{1,3},{2,0},{3,1},{4,6},{5,7},{6,4},{7,5},{8,10},{9,11},{10,... | collective-permute-start | bytes 393224 | tf_op jit(solution)/shard_map/ppermute | solution.py:246
  16.0 0.1 collective-permute-done.8.recv_ref
  16.1 0.7 %write.3.refs_0_ = f32[128,1536]{1,0:T(8,128)} custom-call(f32[1,128,512]{2,1,0:T(8,128)S(1)} %get-tuple-element.48.after.keep_ref, bf16[1,144,512]{2,1,0:T(8,128)(2,1)S(1)} %collective-permute-done.8.recv_ref, f32[1,128,512]{2,1,0:T(8,128)S(1)} %get-tuple-element.60.refs_0_.keep_ref), custom_call_target="tpu_custom_call" | custom-call | flops 1000000 | bytes 1000000 | tf_op jit(solution)/shard_map/write/pallas_call | solution.py:282
  16.9 3.3 %collective-permute-done.7.recv_ref = bf16[1,128,512]{2,1,0:T(8,128)(2,1)S(1)} collective-permute-done((bf16[1,128,512]{2,1,0:T(8,128)(2,1)S(1)}, bf16[1,128,512]{2,1,0:T(8,128)(2,1)S(1)}, u32[]{:S(2)}, u32[]{:S(2)}) %collective-permute-start.7) | collective-permute-done | bytes 131104 | tf_op jit(solution)/shard_map/ppermute | solution.py:246
  20.2 0.8 %write.4.refs_0_ = f32[128,1536]{1,0:T(8,128)} custom-call(f32[1,128,512]{2,1,0:T(8,128)S(1)} %get-tuple-element.62.keep_ref, bf16[1,128,512]{2,1,0:T(8,128)(2,1)S(1)} %collective-permute-done.7.recv_ref, f32[128,1536]{1,0:T(8,128)} %write.3.refs_0_), custom_call_target="tpu_custom_call", output_to_operand_aliasing={{}: (2, {})} | custom-call | flops 10000000000 | bytes 1000000 | tf_op jit(solution)/shard_map/write/pallas_call | solution.py:282
  21.0 1.4 %collective-permute-done.6.recv_ref = bf16[1,128,512]{2,1,0:T(8,128)(2,1)S(1)} collective-permute-done((bf16[1,128,512]{2,1,0:T(8,128)(2,1)S(1)}, bf16[1,128,512]{2,1,0:T(8,128)(2,1)S(1)}, u32[]{:S(2)}, u32[]{:S(2)}) %collective-permute-start.6) | collective-permute-done | bytes 131104 | tf_op jit(solution)/shard_map/ppermute | solution.py:246
  22.4 0.7 %write.5 = f32[128,1536]{1,0:T(8,128)} custom-call(f32[1,128,512]{2,1,0:T(8,128)S(1)} %get-tuple-element.60.refs_0_.keep_ref, bf16[1,128,512]{2,1,0:T(8,128)(2,1)S(1)} %collective-permute-done.6.recv_ref, f32[128,1536]{1,0:T(8,128)} %write.4.refs_0_), custom_call_target="tpu_custom_call", output_to_operand_aliasing={{}: (2, {})} | custom-call | flops 10000000000 | bytes 1000000 | tf_op jit(solution)/shard_map/write/pallas_call | solution.py:282
  (13 shorter events, 0.1 us)
Async XLA Ops:
  0.0 3.4 %copy-start = (bf16[1,8,64,448]{3,2,1,0:T(8,128)(2,1)S(1)}, bf16[1,8,64,448]{3,2,1,0:T(8,128)(2,1)}, u32[]{:S(2)}) copy-start(bf16[1,8,64,448]{3,2,1,0:T(8,128)(2,1)} %param.6) | copy-start | bytes 1376260
  1.8 1.6 %copy-start.1 = (s32[8,128]{1,0:T(8,128)S(1)}, s32[8,128]{1,0:T(8,128)}, u32[]{:S(2)}) copy-start(s32[8,128]{1,0:T(8,128)} %get-tuple-element.35.info_ref) | copy-start | bytes 12292
  1.8 6.9 %collective-permute-start.1 = (bf16[272,256]{1,0:T(8,128)(2,1)}, bf16[272,256]{1,0:T(8,128)(2,1)S(1)}, u32[]{:S(2)}, u32[]{:S(2)}) collective-permute-start(bf16[272,256]{1,0:T(8,128)(2,1)} %get-tuple-element.46), channel_id=1, source_target_pairs={{0,4},{8,12},{16,20},{24,28},{4,0},{12,8},{20,16},{28,24},{1,5},{9... | collective-permute-start | bytes 417800 | tf_op jit(solution)/shard_map/ppermute | solution.py:333
  3.4 2.9 %copy-start.2 = (bf16[1,8,64,256]{3,2,1,0:T(8,128)(2,1)S(1)}, bf16[1,8,64,256]{3,2,1,0:T(8,128)(2,1)}, u32[]{:S(2)}) copy-start(bf16[1,8,64,256]{3,2,1,0:T(8,128)(2,1)} %param.9) | copy-start | bytes 786436
  3.4 8.8 %collective-permute-start.2 = (bf16[272,256]{1,0:T(8,128)(2,1)}, bf16[272,256]{1,0:T(8,128)(2,1)S(1)}, u32[]{:S(2)}, u32[]{:S(2)}) collective-permute-start(bf16[272,256]{1,0:T(8,128)(2,1)} %get-tuple-element.53), channel_id=1, source_target_pairs={{4,8},{12,16},{20,24},{8,4},{16,12},{24,20},{5,9},{13,17},{21,25},... | collective-permute-start | bytes 417800 | tf_op jit(solution)/shard_map/ppermute | solution.py:345
  8.0 1.7 %collective-permute-start = (bf16[2,128,512]{2,1,0:T(8,128)(2,1)S(1)}, bf16[2,128,512]{2,1,0:T(8,128)(2,1)S(1)}, u32[]{:S(2)}, u32[]{:S(2)}) collective-permute-start(bf16[2,128,512]{2,1,0:T(8,128)(2,1)S(1)} %get-tuple-element.37), channel_id=1, source_target_pairs={{0,1},{1,0},{2,3},{3,2},{4,5},{5,4},{6,7},{7,6},{8,9},{9,8},{10,11... | collective-permute-start | bytes 786440 | tf_op jit(solution)/shard_map/ppermute | solution.py:246
  9.8 6.3 %collective-permute-start.8 = (bf16[1,144,512]{2,1,0:T(8,128)(2,1)S(1)}, bf16[1,144,512]{2,1,0:T(8,128)(2,1)S(1)}, u32[]{:S(2)}, u32[]{:S(2)}) collective-permute-start(bf16[1,144,512]{2,1,0:T(8,128)(2,1)S(1)} %get-tuple-element.64), channel_id=1, source_target_pairs={{0,2},{1,3},{2,0},{3,1},{4,6},{5,7},{6,4},{7,5},{8,10},{9,11},{10,... | collective-permute-start | bytes 442376 | tf_op jit(solution)/shard_map/ppermute | solution.py:246
  11.4 2.4 %collective-permute-start.5 = (bf16[2,128,512]{2,1,0:T(8,128)(2,1)S(1)}, bf16[2,128,512]{2,1,0:T(8,128)(2,1)S(1)}, u32[]{:S(2)}, u32[]{:S(2)}) collective-permute-start(bf16[2,128,512]{2,1,0:T(8,128)(2,1)S(1)} %get-tuple-element.58), channel_id=1, source_target_pairs={{0,1},{1,0},{2,3},{3,2},{4,5},{5,4},{6,7},{7,6},{8,9},{9,8},{10,11... | collective-permute-start | bytes 786440 | tf_op jit(solution)/shard_map/ppermute | solution.py:246
  13.2 1.7 %collective-permute-start.3 = (bf16[2,128,256]{2,1,0:T(8,128)(2,1)S(1)}, bf16[2,128,256]{2,1,0:T(8,128)(2,1)S(1)}, u32[]{:S(2)}, u32[]{:S(2)}) collective-permute-start(bf16[2,128,256]{2,1,0:T(8,128)(2,1)S(1)} %get-tuple-element.55), channel_id=1, source_target_pairs={{0,1},{1,0},{2,3},{3,2},{4,5},{5,4},{6,7},{7,6},{8,9},{9,8},{10,11... | collective-permute-start | bytes 393224 | tf_op jit(solution)/shard_map/ppermute | solution.py:246
  13.6 1.4 %collective-permute-start.4 = (bf16[2,128,256]{2,1,0:T(8,128)(2,1)S(1)}, bf16[2,128,256]{2,1,0:T(8,128)(2,1)S(1)}, u32[]{:S(2)}, u32[]{:S(2)}) collective-permute-start(bf16[2,128,256]{2,1,0:T(8,128)(2,1)S(1)} %get-tuple-element.56), channel_id=1, source_target_pairs={{0,1},{1,0},{2,3},{3,2},{4,5},{5,4},{6,7},{7,6},{8,9},{9,8},{10,11... | collective-permute-start | bytes 393224 | tf_op jit(solution)/shard_map/ppermute | solution.py:246
  13.8 6.4 %collective-permute-start.7 = (bf16[1,128,512]{2,1,0:T(8,128)(2,1)S(1)}, bf16[1,128,512]{2,1,0:T(8,128)(2,1)S(1)}, u32[]{:S(2)}, u32[]{:S(2)}) collective-permute-start(bf16[1,128,512]{2,1,0:T(8,128)(2,1)S(1)} %get-tuple-element.63), channel_id=1, source_target_pairs={{0,2},{1,3},{2,0},{3,1},{4,6},{5,7},{6,4},{7,5},{8,10},{9,11},{10,... | collective-permute-start | bytes 393224 | tf_op jit(solution)/shard_map/ppermute | solution.py:246
  15.0 7.4 %collective-permute-start.6 = (bf16[1,128,512]{2,1,0:T(8,128)(2,1)S(1)}, bf16[1,128,512]{2,1,0:T(8,128)(2,1)S(1)}, u32[]{:S(2)}, u32[]{:S(2)}) collective-permute-start(bf16[1,128,512]{2,1,0:T(8,128)(2,1)S(1)} %get-tuple-element.61), channel_id=1, source_target_pairs={{0,2},{1,3},{2,0},{3,1},{4,6},{5,7},{6,4},{7,5},{8,10},{9,11},{10,... | collective-permute-start | bytes 393224 | tf_op jit(solution)/shard_map/ppermute | solution.py:246
